TPU v7x, 256 devices: a whole 4x4x8 slice. The times are simulated.
256 devices in a mesh: grp: 2 (over x_hi), tp: 64 (over y, x_lo, z), seq: 2 (over core).
Axes of the slice: x: 4 (x_hi: 2, x_lo: 2; x = x_hi * 2 + x_lo), y: 4, z: 8, core: 2. Of those that a mesh axis runs over, the one named last changes fastest.
Arguments:
- feats: bfloat16 [256, 3, 8192], P('seq', None, 'tp'), may hold values from -6 to 6
- ids: int32 [256], replicated, may hold values from 0 to 16383
- loss_mask: int32 [256], replicated, may hold values 0 or 1
- owner: int32 [16, 1], replicated, may hold values from 0 to 1; in each aligned block of 8 rows (0 to 7, 8 to 15, ...) at most 6 rows name the same one
- shifts: int32 [3], replicated, may hold values from 0 to 15
- target_gain: bfloat16 [8192], replicated, may hold values from 0.5 to 1.5
- target_head: bfloat16 [8192, 16384], P(None, ('grp', 'tp')), may hold values from -16 to 16
- fc_weight: bfloat16 [24576, 8192], P('grp', 'tp'), may hold values from -0.0390625 to 0.0390625
- embed: bfloat16 [16384, 8192], P('grp', 'tp'), may hold values from -6 to 6
- draft_gain: bfloat16 [8192], replicated, may hold values from 0.5 to 1.5
- layer_weight: bfloat16 [8192, 8192], P(None, 'tp'), may hold values from -0.0625 to 0.0625
- draft_head: bfloat16 [8192, 16384], P(None, ('grp', 'tp')), may hold values from -16 to 16
Outputs:
- head_grad: bfloat16 [8192, 16384], P('seq', ('grp', 'tp'))
- slot_kl: float32 [3, 384], P(None, 'seq')
Inputs may be any that keep to these rules, and one draw needn't show every extreme that they name: Among the blocks of one seq index (aligned blocks of 8 rows) no owner is named more than 6 times, a bound that some block reaches.
All inputs are finite; a program needn't handle non-finite values.
Results may differ from a plain program's by a relative error of at most 0.039.
The roundings to bfloat16 on the way count: a program that leaves them out, or rounds other values in their place, can miss the bound.
Values may be sent and summed in bfloat16 or wider, within the bound.
No kernel may reach another device: no remote copies, remote signals or barrier semaphores. Data moves between devices by JAX's collectives and lax.ppermute only.
A program may use at most 128 MiB of HBM per device.

v0:
```python
import jax
import jax.numpy as jnp
from jax import lax
from jax.sharding import PartitionSpec as P

BLK = 16
STEPS = 3
MOST = 6


def normalize(values):
    return values * lax.rsqrt(jnp.mean(values * values, axis=-1, keepdims=True) + 1e-05)


def entropy_part(target):
    positive = target > 0
    return jnp.where(positive, target * jnp.log(jnp.where(positive, target, 1.0)), 0.0)


def width_rows(values):
    return lax.all_gather(values, "tp", axis=1, tiled=True)


def group_sums(united_part, embed_part):
    return lax.psum((united_part, embed_part), "grp")


def route_blocks(first_load, second_load):
    return (
        lax.all_to_all(first_load, "seq", split_axis=0, concat_axis=0, tiled=True),
        lax.all_to_all(second_load, "seq", split_axis=0, concat_axis=0, tiled=True),
    )


def vocab_totals(logits, extra_one, extra_two):
    local_peak = jnp.max(logits, axis=1)
    peak_val = lax.pmax(local_peak, ("grp", "tp"))
    totals = jnp.sum(jnp.exp(logits - peak_val[:, None]), axis=1)
    summed = lax.psum((totals, extra_one, extra_two), ("grp", "tp"))
    return (peak_val, summed[0], summed[1], summed[2])


def embed_steps(block_ids, ids, shifts, embed, group_index):
    offsets = (jnp.arange(BLK, dtype=jnp.int32)[None, :] + shifts[:, None]) % BLK
    row_index = block_ids[:, None, None] * BLK + offsets[None, :, :]
    token_ids = jnp.take(ids, row_index, axis=0)
    local_ids = token_ids - group_index * embed.shape[0]
    inside = (local_ids >= 0) & (local_ids < embed.shape[0])
    picked = jnp.take(embed, jnp.clip(local_ids, 0, embed.shape[0] - 1), axis=0)
    return jnp.where(inside[..., None], picked.astype(jnp.float32), 0.0)


def on_device(
    feats,
    ids,
    loss_mask,
    owner,
    shifts,
    target_gain,
    target_head,
    fc_weight,
    embed,
    draft_gain,
    layer_weight,
    draft_head,
):
    seq_count = lax.axis_size("seq")
    seq_index = lax.axis_index("seq")
    group_index = lax.axis_index("grp")
    vocab_total = draft_head.shape[1] * lax.axis_size("grp") * lax.axis_size("tp")
    tok_dev, levels, width_dev = feats.shape
    full_width = target_gain.shape[0]
    block_count = tok_dev // BLK
    slot_rows = seq_count * MOST * BLK
    owners = owner[:, 0].reshape(seq_count, block_count)
    seq_ids = jnp.arange(seq_count, dtype=jnp.int32)
    owner_hits = (owners[:, :, None] == seq_ids[None, None, :]).astype(jnp.int32)
    owner_rank = jnp.sum((jnp.cumsum(owner_hits, axis=1) - 1) * owner_hits, axis=2)
    self_owner = lax.dynamic_index_in_dim(owners, seq_index, 0, keepdims=False)
    self_rank = lax.dynamic_index_in_dim(owner_rank, seq_index, 0, keepdims=False)
    slot_target = self_owner * MOST + self_rank
    picker = (
        jnp.arange(seq_count * MOST, dtype=jnp.int32)[:, None] == slot_target[None, :]
    ).astype(jnp.bfloat16)
    matches = (owners[:, None, :] == seq_index) & (
        owner_rank[:, None, :] == jnp.arange(MOST, dtype=jnp.int32)[None, :, None]
    )
    block_index = seq_ids[:, None] * block_count + jnp.arange(block_count, dtype=jnp.int32)[None, :]
    slot_block = jnp.sum(jnp.where(matches, block_index[:, None, :], 0), axis=2).reshape(-1)
    slot_live = jnp.sum(matches.astype(jnp.int32), axis=2).reshape(-1)
    token_index = (slot_block[:, None] * BLK + jnp.arange(BLK, dtype=jnp.int32)[None, :]).reshape(
        -1
    )
    live_rows = (slot_live[:, None] * jnp.ones((1, BLK), jnp.int32)).reshape(-1).astype(jnp.float32)
    mask_rows = jnp.take(loss_mask, token_index, axis=0).astype(jnp.float32) * live_rows
    weights = mask_rows * (vocab_total / (STEPS * BLK))
    high_rows = width_rows(feats[:, 2, :])
    target_rows = (
        normalize(high_rows.astype(jnp.float32)) * target_gain.astype(jnp.float32)
    ).astype(jnp.bfloat16)
    target_logits = jnp.dot(target_rows, target_head, preferred_element_type=jnp.float32)
    zero_rows = jnp.zeros((tok_dev,), jnp.float32)
    target_peak, target_totals, unused_one, unused_two = vocab_totals(
        target_logits, zero_rows, zero_rows
    )
    target_probs = (jnp.exp(target_logits - target_peak[:, None]) / target_totals[:, None]).astype(
        jnp.bfloat16
    )

    def select_slots(payload):
        return jnp.dot(picker, payload, preferred_element_type=jnp.float32).astype(jnp.bfloat16)

    half_rows = fc_weight.shape[0]
    arrived, arrived_probs = route_blocks(
        select_slots(feats.reshape(block_count, -1)),
        select_slots(target_probs.reshape(block_count, -1)),
    )
    wide_rows = width_rows(arrived.reshape(slot_rows * levels, width_dev)).reshape(
        slot_rows, levels * full_width
    )
    united_part = jnp.dot(
        lax.dynamic_slice_in_dim(wide_rows, group_index * half_rows, half_rows, 1),
        fc_weight,
        preferred_element_type=jnp.float32,
    )
    united_sum, embed_rows = group_sums(
        united_part, embed_steps(slot_block, ids, shifts, embed, group_index)
    )
    united_rows = united_sum.astype(jnp.bfloat16)
    probs_blocks = arrived_probs.reshape(seq_count * MOST, BLK, -1)
    hidden_state = united_rows.astype(jnp.float32)
    total_grad = jnp.zeros((full_width, draft_head.shape[1]), jnp.float32)
    scores = []
    for turn_index in range(STEPS):
        mixed = (hidden_state + embed_rows[:, turn_index].reshape(slot_rows, width_dev)).astype(
            jnp.bfloat16
        )
        gathered = width_rows(mixed)
        normed = (normalize(gathered.astype(jnp.float32)) * draft_gain.astype(jnp.float32)).astype(
            jnp.bfloat16
        )
        if turn_index + 1 < STEPS:
            hidden_state = hidden_state + jax.nn.silu(
                jnp.dot(normed, layer_weight, preferred_element_type=jnp.float32)
            )
        logits = jnp.dot(normed, draft_head, preferred_element_type=jnp.float32)
        shift_order = (jnp.arange(BLK, dtype=jnp.int32) + shifts[turn_index]) % BLK
        target = (
            jnp.take(probs_blocks, shift_order, axis=1).reshape(slot_rows, -1).astype(jnp.float32)
        )
        cross_term = jnp.sum(entropy_part(target) - target * logits, axis=1)
        prob_mass = jnp.sum(target, axis=1)
        peak_val, totals, cross_term, prob_mass = vocab_totals(logits, cross_term, prob_mass)
        kl_terms = cross_term + (peak_val + jnp.log(totals)) * prob_mass
        soft_probs = jnp.exp(logits - peak_val[:, None]) / totals[:, None]
        grad_logits = (weights[:, None] * (soft_probs * prob_mass[:, None] - target)).astype(
            jnp.bfloat16
        )
        total_grad = total_grad + jnp.dot(normed.T, grad_logits, preferred_element_type=jnp.float32)
        scores.append(kl_terms * mask_rows)
    head_grad = lax.psum_scatter(total_grad, "seq", scatter_dimension=0, tiled=True).astype(
        jnp.bfloat16
    )
    return (head_grad, jnp.stack(scores))


def solution(mesh):
    return jax.shard_map(
        on_device,
        mesh=mesh,
        in_specs=(
            P("seq", None, "tp"),
            P(),
            P(),
            P(),
            P(),
            P(),
            P(None, ("grp", "tp")),
            P("grp", "tp"),
            P("grp", "tp"),
            P(),
            P(None, "tp"),
            P(None, ("grp", "tp")),
        ),
        out_specs=(P("seq", ("grp", "tp")), P(None, "seq")),
        check_vma=False,
    )
```

profile of v0, /device:TPU:1, one launch (start us, length us, event | category | flops | bytes accessed | tf_op | source)
XLA Modules:
  0.0 2383.6 jit_solution(12032392836619963769)
XLA Ops:
  11.9 3.9 gather_fusion
  16.4 3.5 gather_fusion.1
  22.0 6.8 all_to_all.18
  29.7 34.5 %all-reduce.4.cloned.1.call-done = f32[12,3,16,128]{3,2,0,1:T(8,128)} async-done(((f32[12,3,16,128]{3,2,0,1:T(8,128)}), f32[12,3,16,128]{3,2,0,1:T(8,128)}) %all-reduce.4.cloned.1.call-update) | async-done | bytes 294928 | tf_op jit(solution)/shard_map/psum | solution.py:25
  65.2 203.1 %all-gather.7.cloned.1.call-done = bf16[576,8192]{1,0:T(8,128)(2,1)} async-done(((bf16[576,128]{1,0:T(8,128)(2,1)}), bf16[576,8192]{1,0:T(8,128)(2,1)}) %all-gather.7.cloned.1.call-update) | async-done | bytes 9437200 | tf_op jit(solution)/shard_map/all_gather | solution.py:21
  268.4 12.9 reshape.285
  281.2 4.4 fusion.9
  285.6 11.8 psum.84
  298.2 237.9 %all-gather.9.cloned.1.call-done = bf16[192,8192]{1,0:T(8,128)(2,1)} async-done(((bf16[192,128]{1,0:T(8,128)(2,1)}), bf16[192,8192]{1,0:T(8,128)(2,1)}) %all-gather.9.cloned.1.call-update) | async-done | bytes 3145744 | tf_op jit(solution)/shard_map/all_gather | solution.py:21
  536.0 2.8 fusion
  538.9 3.4 fusion.40
  543.8 234.7 %all-gather.11.cloned.1.call-done = bf16[192,8192]{1,0:T(8,128)(2,1)} async-done(((bf16[192,128]{1,0:T(8,128)(2,1)}), bf16[192,8192]{1,0:T(8,128)(2,1)}) %all-gather.11.cloned.1.call-update) | async-done | bytes 3145744 | tf_op jit(solution)/shard_map/all_gather | solution.py:21
  781.3 3.5 fusion.37
  794.4 216.4 %all-gather.15.cloned.1.call-done = bf16[128,1,8192]{2,0,1:T(8,128)(2,1)} async-done(((bf16[128,1,128]{2,0,1:T(8,128)(2,1)}), bf16[128,1,8192]{2,0,1:T(8,128)(2,1)}) %all-gather.15.cloned.1.call-update) | async-done | bytes 2097168 | tf_op jit(solution)/shard_map/all_gather | solution.py:21
  1013.0 3.3 fusion.82
  1020.1 230.0 %all-gather.13.cloned.1.call-done = bf16[192,8192]{1,0:T(8,128)(2,1)} async-done(((bf16[192,128]{1,0:T(8,128)(2,1)}), bf16[192,8192]{1,0:T(8,128)(2,1)}) %all-gather.13.cloned.1.call-update) | async-done | bytes 3145744 | tf_op jit(solution)/shard_map/all_gather | solution.py:21
  1252.9 3.4 fusion.85
  1256.4 292.2 %all-reduce.1 = (f32[128]{0:T(128)S(1)}, f32[192]{0:T(256)S(1)}, f32[192]{0:T(256)S(1)}, f32[192]{0:T(256)S(1)}) all-reduce(f32[128]{0:T(128)S(1)} %get-tuple-element.40, f32[192]{0:T(256)S(1)} %get-tuple-element.42, f32[192]{0:T(256)S(1)} %get-tuple-element.46, ...), channel_id=1, replica_groups=mesh['grp'=2,'tp'=64,'seq'=2] {'grp','tp'}, use_global_device_ids=true, to_apply=%region_13.14 | all-reduce | flops 704 | bytes 5632 | tf_op jit(solution)/shard_map/pmax | solution.py:37
  1548.7 287.1 %psum.87 = f32[128]{0:T(128)S(1)} all-reduce(f32[128]{0:T(128)S(1)} %fusion.46), channel_id=1, replica_groups=mesh['grp'=2,'tp'=64,'seq'=2] {'grp','tp'}, use_global_device_ids=true, to_apply=%region_15.16 | all-reduce | flops 128 | bytes 1024 | tf_op jit(solution)/shard_map/psum | solution.py:39
  1836.1 151.1 %all_to_all.19 = bf16[2,6,2048]{2,1,0:T(8,128)(2,1)S(1)} all-to-all(bf16[2,6,2048]{2,1,0:T(8,128)(2,1)S(1)} %all_to_all.14), channel_id=1, replica_groups=mesh['grp'=2,'tp'=64,'seq'=2] {'seq'}, dimensions={0} | all-to-all | bytes 98304 | tf_op jit(solution)/shard_map/all_to_all | solution.py:31
  2000.9 297.2 %all-reduce = (f32[192]{0:T(256)S(1)}, f32[192]{0:T(256)S(1)}, f32[192]{0:T(256)S(1)}, f32[192]{0:T(256)S(1)}, f32[192]{0:T(256)S(1)}, /*index=5*/f32[192]{0:T(2...) all-reduce(f32[192]{0:T(256)} %reduce_sum.167, ...), channel_id=1, replica_groups=mesh['grp'=2,'tp'=64,'seq'=2] {'grp','tp'}, use_global_device_ids=true, to_apply=%region_17.19 | all-reduce | flops 1728 | bytes 13824 | tf_op jit(solution)/shard_map/psum | solution.py:39
  2300.2 3.6 fusion.75
  2305.6 3.7 convolution_add_fusion
  2309.9 63.4 %reduce-scatter.2.cloned.1.call-done = f32[4096,128]{1,0:T(8,128)} async-done(((f32[8192,128]{1,0:T(8,128)}), f32[4096,128]{1,0:T(8,128)}) %reduce-scatter.2.cloned.1.call-update) | async-done | bytes 2097168 | tf_op jit(solution)/shard_map/reduce_scatter | solution.py:161
  (163 shorter events, 52.8 us)
Async XLA Ops:
  8.0 273.2 %copy-start = (bf16[12288,128]{1,0:T(8,128)(2,1)S(1)}, bf16[12288,128]{1,0:T(8,128)(2,1)}, u32[]{:S(2)}) copy-start(bf16[12288,128]{1,0:T(8,128)(2,1)} %param.21) | copy-start | bytes 9437188
  8.0 3.9 copy-start.1
  8.0 56.2 %all-reduce.4.cloned.1.call-start = ((), (), s32[]{:S(2)}) async-start(), calls=%async_computation.4 | async-start | bytes 589824 | tf_op jit(solution)/shard_map/psum | solution.py:25
  11.9 9.1 copy-start.11
  20.9 247.4 %all-gather.7.cloned.1.call-start = ((), (), s32[]{:S(2)}) async-start(), calls=%async_computation.3 | async-start | bytes 9584640 | tf_op jit(solution)/shard_map/all_gather | solution.py:21
  29.7 506.3 %all-gather.9.cloned.1.call-start = ((), (), s32[]{:S(2)}) async-start(), calls=%async_computation.5 | async-start | bytes 3194880 | tf_op jit(solution)/shard_map/all_gather | solution.py:21
  281.2 16.9 copy-start.12
  298.1 480.4 %all-gather.11.cloned.1.call-start = ((), (), s32[]{:S(2)}) async-start(), calls=%async_computation.6 | async-start | bytes 3194880 | tf_op jit(solution)/shard_map/all_gather | solution.py:21
  536.0 2.8 copy-start.8
  542.3 239.0 %copy-start.23 = (f32[192,128]{1,0:T(8,128)S(1)}, f32[192,128]{1,0:T(8,128)}, u32[]{:S(2)}) copy-start(f32[192,128]{1,0:T(8,128)} %get-tuple-element.45) | copy-start | bytes 294916
  542.3 468.4 %all-gather.15.cloned.1.call-start = ((), (), s32[]{:S(2)}) async-start(), calls=%async_computation.9 | async-start | bytes 2129920 | tf_op jit(solution)/shard_map/all_gather | solution.py:21
  543.7 706.4 %all-gather.13.cloned.1.call-start = ((), (), s32[]{:S(2)}) async-start(), calls=%async_computation.7 | async-start | bytes 3194880 | tf_op jit(solution)/shard_map/all_gather | solution.py:21
  781.2 236.9 %copy-start.14 = (f32[192]{0:T(256)}, f32[192]{0:T(256)S(1)}, u32[]{:S(2)}) copy-start(f32[192]{0:T(256)S(1)} %add_rsqrt_fusion.1) | copy-start | bytes 2308
  781.3 5.4 copy-start.13
  781.3 5.4 copy-start.2
  781.3 7.6 copy-start.18
  784.8 1588.5 %reduce-scatter.2.cloned.1.call-start = ((), (), s32[]{:S(2)}) async-start(), calls=%async_computation.8 | async-start | bytes 6291456 | tf_op jit(solution)/shard_map/reduce_scatter | solution.py:161
  790.1 1198.7 %copy-start.21 = (pred[16]{0:T(512)(128)(4,1)}, pred[16]{0:T(512)(128)(4,1)S(1)}, u32[]{:S(2)}) copy-start(pred[16]{0:T(512)(128)(4,1)S(1)} %compare_and_fusion.5) | copy-start | bytes 52
  1010.8 5.6 copy-start.9
  1010.8 5.6 copy-start.22
  1252.9 3.4 copy-start.16
  1252.9 583.0 %copy-start.20 = (s32[8]{0:T(128)S(1)}, s32[8]{0:T(128)}, u32[]{:S(2)}) copy-start(s32[8]{0:T(128)} %copy-done.19) | copy-start | bytes 100
  2300.1 3.6 copy-start.5
  2300.2 3.6 copy-start.15
  (7 other events, 12.5 us)
Sparse Core Ops, SparseCore 0:
  21.0 43.1 all-reduce.3
  2309.4 63.8 reduce-scatter.1
Sparse Core Ops, SparseCore 1:
  29.8 238.5 all-gather.6
  298.2 237.8 all-gather.8
  542.4 236.0 all-gather.10
  780.2 230.5 all-gather.14
  1013.1 237.0 all-gather.12
where the time goes:
time: 2380 us
  waiting for transfers between devices  1220 us (51%)
  blocking collectives  1050 us (44%)
  local copies, waits for them, and re-layouts  36.9 us (2%)
  other arithmetic  32.8 us (1%)
  matrix products  30.9 us (1%)
    all_gather x5, waiting for transfers between devices, width_rows(): return lax.all_gather(values, 'tp', axis=1, tiled=True)  1120 us
    psum x2, blocking collectives, vocab_totals(): summed = lax.psum((totals, extra_one, extra_two), ('grp', 'tp'))  584 us
    pmax x1, blocking collectives, vocab_totals(): peak_val = lax.pmax(local_peak, ('grp', 'tp'))  292 us
    all_to_all x1, blocking collectives, route_blocks(): lax.all_to_all(second_load, 'seq', split_axis=0, concat_axis=0, tiled=True)  151 us
    reduce_scatter x1, waiting for transfers between devices, on_device(): lax.psum_scatter(total_grad, 'seq', scatter_dimension=0, tiled=True)  63.4 us
  transfers between devices with their start and end apart: 7, of which 7 were waited for; matrix products, arithmetic and copies ran while one was open for 1% of the time, Pallas kernels for 0%

commit v1 on v0

v1 whole, which is shorter than its diff:
```python
import functools

import jax
import jax.numpy as jnp
import numpy as np
from jax import lax
from jax.experimental import pallas as pl
from jax.experimental.pallas import tpu as pltpu
from jax.sharding import Mesh
from jax.sharding import PartitionSpec as P

BLK = 16
STEPS = 3
MOST = 6
LANE = 128
HALF = 64
TOK = 128
EPS = 1e-05

VMEM = pl.BlockSpec(memory_space=pltpu.VMEM)
SMEM = pl.BlockSpec(memory_space=pltpu.SMEM)
F32 = jnp.float32
BF16 = jnp.bfloat16


def call(kernel, outs, ins, *, flops=0, nbytes=0, scratch=()):
    return pl.pallas_call(
        kernel,
        out_shape=outs,
        in_specs=list(ins),
        out_specs=jax.tree.map(lambda _: VMEM, outs),
        scratch_shapes=list(scratch),
        compiler_params=pltpu.CompilerParams(vmem_limit_bytes=48 * 1024 * 1024),
        cost_estimate=pl.CostEstimate(flops=flops, bytes_accessed=nbytes, transcendentals=0),
    )


def sds(shape, dtype):
    return jax.ShapeDtypeStruct(shape, dtype)


def dot(a, b):
    return jnp.dot(a, b, preferred_element_type=F32)


def spread(values, axis):
    count = lax.axis_size(axis)
    return lax.all_to_all(
        jnp.broadcast_to(values[None], (count,) + values.shape), axis, 0, 0, tiled=True
    )


def swap(values, axis):
    count = lax.axis_size(axis)
    return lax.ppermute(values, axis, [(i, (i + count // 2) % count) for i in range(count)])


def shift_matrix(shift, rows):
    src = lax.broadcasted_iota(jnp.int32, (rows, rows), 0)
    tok = lax.broadcasted_iota(jnp.int32, (rows, rows), 1)
    want = (tok & ~(BLK - 1)) + ((tok & (BLK - 1)) + shift & (BLK - 1))
    return jnp.where(src == want, 1.0, 0.0).astype(BF16)


def shift_rows(shift, rows):
    tok = lax.broadcasted_iota(jnp.int32, (rows, rows), 0)
    src = lax.broadcasted_iota(jnp.int32, (rows, rows), 1)
    want = (tok & ~(BLK - 1)) + ((tok & (BLK - 1)) + shift & (BLK - 1))
    return jnp.where(src == want, 1.0, 0.0).astype(BF16)


def split3(x):
    hi = x.astype(BF16)
    rest = x - hi.astype(F32)
    mid = rest.astype(BF16)
    low = (rest - mid.astype(F32)).astype(BF16)
    return hi, mid, low


def unite_kernel(pos_ref, x_ref, fc_ref, own_ref, other_ref, acc_ref):
    g = pos_ref[0]
    whole = pl.multiple_of(g * 4096, 4096)
    middle = pl.multiple_of((1 - g) * 8192, 4096)
    acc = jnp.zeros((TOK, LANE), F32)
    for i in range(4):
        lhs = jnp.concatenate([x_ref[i * 16 + j, 0:TOK, :] for j in range(16)], axis=1)
        acc += dot(lhs, fc_ref[pl.ds(whole + i * 2048, 2048), :])
    acc_ref[...] = acc
    for h in range(2):
        part = jnp.zeros((HALF, LANE), F32)
        for i in range(2):
            lhs = jnp.concatenate(
                [x_ref[h * 32 + i * 16 + j, TOK : TOK + HALF, :] for j in range(16)], axis=1
            )
            part += dot(lhs, fc_ref[pl.ds(middle + i * 2048, 2048), :])
        acc_ref[h * HALF : (h + 1) * HALF, :] += part
    own_ref[...] = acc_ref[pl.ds(pl.multiple_of(g * HALF, HALF), HALF), :]
    other_ref[...] = acc_ref[pl.ds(pl.multiple_of((1 - g) * HALF, HALF), HALF), :]


def first_kernel(shifts_ref, own_ref, got_ref, e_own_ref, e_got_ref, state_ref, e_ref, mix_ref):
    state = (own_ref[...] + got_ref[...]).astype(BF16).astype(F32)
    state_ref[...] = state
    rows = (e_own_ref[...].astype(F32) + e_got_ref[...].astype(F32)).astype(BF16)
    e_ref[...] = rows
    mixed = (state + dot(shift_rows(shifts_ref[0], HALF), rows)).astype(BF16)
    for i in range(8):
        mix_ref[i] = mixed


def normalize_into(x_of, gain_ref, count, rows, out_of):
    total = jnp.zeros((rows, LANE), F32)
    for p in range(count):
        v = x_of(p).astype(F32)
        total += v * v
    scale = lax.rsqrt(jnp.sum(total, axis=1, keepdims=True) / (count * LANE) + EPS)
    for i in range(count // 16):
        gain = gain_ref[i].astype(F32)
        for j in range(16):
            p = i * 16 + j
            out_of(p, (x_of(p).astype(F32) * scale * gain[j : j + 1, :]).astype(BF16))


def row_dot(n_of, w_ref, rows):
    acc = jnp.zeros((rows, LANE), F32)
    for i in range(4):
        lhs = jnp.concatenate([n_of(i * 16 + j) for j in range(16)], axis=1)
        acc += dot(lhs, w_ref[i * 2048 : (i + 1) * 2048, :])
    return acc


def layer_kernel(step, shifts_ref, x_ref, gain_ref, w_ref, state_ref, e_ref, n_ref, next_ref, mix_ref):
    def put(p, value):
        n_ref[p] = value

    normalize_into(lambda p: x_ref[p], gain_ref, 64, HALF, put)
    acc = row_dot(lambda p: n_ref[p], w_ref, HALF)
    state = state_ref[...] + acc * jax.nn.sigmoid(acc)
    next_ref[...] = state
    mixed = (state + dot(shift_rows(shifts_ref[step + 1], HALF), e_ref[...])).astype(BF16)
    for i in range(mix_ref.shape[0]):
        mix_ref[i] = mixed


def target_kernel(x_ref, gain_ref, w_ref, logits_ref, stat_ref, n_ref):
    def put(p, value):
        n_ref[p] = value

    normalize_into(lambda p: x_ref[p], gain_ref, 64, TOK, put)
    logits = row_dot(lambda p: n_ref[p], w_ref, TOK).T
    logits_ref[...] = logits
    peak = jnp.max(logits, axis=0, keepdims=True)
    total = jnp.sum(jnp.exp(logits - peak), axis=0, keepdims=True)
    parts = list(split3(peak)) + list(split3(total))
    rows = jnp.concatenate(
        [v.astype(F32) for v in parts] + [jnp.zeros((10, LANE), F32)], axis=0
    )
    stat_ref[...] = rows.astype(BF16)


def logits_kernel(
    pos_ref,
    shifts_ref,
    x_ref,
    tstat_ref,
    gain_ref,
    w_ref,
    a0_ref,
    b0_ref,
    a1_ref,
    b1_ref,
    t_ref,
    n_ref,
    l_ref,
    p_ref,
    stat_ref,
    rows_ref,
):
    g = pos_ref[0]
    for h in range(2):

        def put(p, value, h=h):
            n_ref[p, h * HALF : (h + 1) * HALF, :] = value

        normalize_into(lambda p, h=h: x_ref[h, p], gain_ref, 64, HALF, put)
    peaks = tstat_ref[:, 0].astype(F32) + tstat_ref[:, 1].astype(F32) + tstat_ref[:, 2].astype(F32)
    totals = tstat_ref[:, 3].astype(F32) + tstat_ref[:, 4].astype(F32) + tstat_ref[:, 5].astype(F32)
    peak = jnp.max(peaks, axis=0, keepdims=True)
    total = jnp.sum(totals * jnp.exp(peaks - peak), axis=0, keepdims=True)
    probs = (jnp.exp(t_ref[...] - peak) / total).astype(BF16)
    own = pl.ds(pl.multiple_of(g * HALF, HALF), HALF)
    other = pl.ds(pl.multiple_of((1 - g) * HALF, HALF), HALF)
    stats = []
    for k in range(STEPS):
        if k == 2:
            logits = row_dot(lambda p: n_ref[p], w_ref, TOK)
        else:
            mine, theirs = ((a0_ref, b0_ref), (a1_ref, b1_ref))[k]
            rows_ref[own, :] = row_dot(lambda p: mine[p], w_ref, HALF)
            rows_ref[other, :] = row_dot(lambda p: theirs[p], w_ref, HALF)
            logits = rows_ref[...]
        logits = logits.T
        l_ref[k] = logits
        target = dot(probs, shift_matrix(shifts_ref[k], TOK))
        p_ref[k] = target.astype(BF16)
        peak = jnp.max(logits, axis=0, keepdims=True)
        total = jnp.sum(jnp.exp(logits - peak), axis=0, keepdims=True)
        positive = target > 0
        entropy = jnp.where(positive, target * jnp.log(jnp.where(positive, target, 1.0)), 0.0)
        cross = jnp.sum(entropy - target * logits, axis=0, keepdims=True)
        mass = jnp.sum(target, axis=0, keepdims=True)
        stats += [peak, total, cross, mass]
    rows = jnp.concatenate(stats + [jnp.zeros((4, LANE), F32)], axis=0)
    for i in range(8):
        stat_ref[i] = rows


def combine(blocks):
    rows = []
    for k in range(STEPS):
        peaks = blocks[:, 4 * k, :]
        peak = jnp.max(peaks, axis=0, keepdims=True)
        total = jnp.sum(blocks[:, 4 * k + 1, :] * jnp.exp(peaks - peak), axis=0, keepdims=True)
        cross = jnp.sum(blocks[:, 4 * k + 2, :], axis=0, keepdims=True)
        mass = jnp.sum(blocks[:, 4 * k + 3, :], axis=0, keepdims=True)
        rows.append((peak, total, cross, mass))
    return rows


def middle_kernel(in_ref, out_ref):
    rows = []
    for item in combine(in_ref[...]):
        rows += list(item)
    rows = jnp.concatenate(rows + [jnp.zeros((4, LANE), F32)], axis=0)
    for i in range(16):
        out_ref[i] = rows


def grad_kernel(vocab_total, pos_ref, in_ref, mask_ref, l_ref, p_ref, grad_ref, kl_ref):
    g = pos_ref[0]
    mask = mask_ref[...]
    weight = mask * (vocab_total / (STEPS * BLK))
    scores = []
    for k, (peak, total, cross, mass) in enumerate(combine(in_ref[...])):
        soft = jnp.exp(l_ref[k] - peak) / total
        grad = weight * (soft * mass - p_ref[k].astype(F32))
        if k < 2:
            grad = pltpu.roll(grad, g * HALF, 1)
        grad_ref[k] = grad.astype(BF16)
        scores.append((cross + (peak + jnp.log(total)) * mass) * mask)
    kl_ref[...] = jnp.concatenate(scores + [jnp.zeros((5, LANE), F32)], axis=0)


def head_kernel(
    pos_ref, g_ref, h_ref, a0_ref, b0_ref, a1_ref, b1_ref, n2_ref, c0_ref, d0_ref, c1_ref, d1_ref, m2_ref, out_ref
):
    first = pos_ref[1] * 32
    lhs = jnp.concatenate(
        [g_ref[0], g_ref[1], g_ref[2], h_ref[0], h_ref[1], h_ref[2]], axis=1
    )

    def body(q, carry):
        p = first + q
        rhs = jnp.concatenate(
            [
                a0_ref[p],
                b0_ref[p],
                a1_ref[p],
                b1_ref[p],
                n2_ref[p],
                c0_ref[q],
                d0_ref[q],
                c1_ref[q],
                d1_ref[q],
                m2_ref[q],
            ],
            axis=0,
        )
        out_ref[q] = dot(lhs, rhs).T.astype(BF16)
        return carry

    lax.fori_loop(0, 32, body, 0, unroll=4)


def on_device(
    feats,
    ids,
    loss_mask,
    owner,
    shifts,
    target_gain,
    target_head,
    fc_weight,
    embed,
    draft_gain,
    layer_weight,
    draft_head,
):
    g = lax.axis_index("xh")
    c = lax.axis_index("c")
    y_half = lax.axis_index("y") // 2
    pos = jnp.stack([g, c]).astype(jnp.int32)
    vocab_total = LANE * 128
    target_gain = target_gain.reshape(4, 16, LANE)
    draft_gain = draft_gain.reshape(4, 16, LANE)

    mid = feats[:, 1, :].reshape(2, HALF, LANE)
    mid_own = lax.dynamic_index_in_dim(mid, y_half, 0, keepdims=False)
    mid_send = lax.dynamic_index_in_dim(mid, 1 - y_half, 0, keepdims=False)
    mid_got = swap(mid_send, "y")

    seq_ids = lax.dynamic_slice_in_dim(ids, c * TOK, TOK, 0)
    local_ids = seq_ids - g * embed.shape[0]
    inside = (local_ids >= 0) & (local_ids < embed.shape[0])
    picked = jnp.take(embed, jnp.clip(local_ids, 0, embed.shape[0] - 1), axis=0)
    picked = jnp.where(inside[:, None], picked, jnp.zeros((), BF16)).reshape(2, HALF, LANE)
    e_own = lax.dynamic_index_in_dim(picked, g, 0, keepdims=False)
    e_got = swap(lax.dynamic_index_in_dim(picked, 1 - g, 0, keepdims=False), "xh")

    level = jnp.where(g == 0, feats[:, 0, :], feats[:, 2, :])
    piece = jnp.where(y_half == g, mid_own, mid_got)
    load = jnp.concatenate([level, piece], axis=0)
    wide = spread(load, "z").reshape(8 * 192, LANE)
    wide = spread(wide, ("y", "xl")).reshape(64, 192, LANE)

    own_part, other_part = call(
        unite_kernel,
        (sds((HALF, LANE), F32), sds((HALF, LANE), F32)),
        (SMEM, VMEM, VMEM),
        flops=2 * 128 * 12288 * 128,
        nbytes=6 << 20,
        scratch=[pltpu.VMEM((TOK, LANE), F32)],
    )(pos, wide, fc_weight)
    part_got = swap(other_part, "xh")

    high_own = wide[:, :TOK, :]
    high_got = lax.ppermute(high_own, "xh", [(1, 0)])

    state, e_rows, mix = call(
        first_kernel,
        (sds((HALF, LANE), F32), sds((HALF, LANE), BF16), sds((8, HALF, LANE), BF16)),
        (SMEM, VMEM, VMEM, VMEM, VMEM),
    )(shifts, own_part, part_got, e_own, e_got)

    mine, theirs = [], []
    for step in range(2):
        part = lax.all_to_all(mix, "z", 0, 0, tiled=True).reshape(8 * HALF, LANE)
        rows = spread(part, ("y", "xl")).reshape(64, HALF, LANE)
        normed, state, mix = call(
            functools.partial(layer_kernel, step),
            (
                sds((64, HALF, LANE), BF16),
                sds((HALF, LANE), F32),
                sds((8 if step == 0 else 1, HALF, LANE), BF16),
            ),
            (SMEM, VMEM, VMEM, VMEM, VMEM, VMEM),
            flops=2 * 64 * 8192 * 128,
            nbytes=4 << 20,
        )(shifts, rows, draft_gain, layer_weight, state, e_rows)
        mine.append(normed)
        theirs.append(swap(normed, "xh"))

    high = jnp.where(g == 0, high_got, high_own)
    t_logits, t_stat = call(
        target_kernel,
        (sds((LANE, TOK), F32), sds((16, LANE), BF16)),
        (VMEM, VMEM, VMEM),
        flops=2 * 128 * 8192 * 128,
        nbytes=4 << 20,
        scratch=[pltpu.VMEM((64, TOK, LANE), BF16)],
    )(high, target_gain, target_head)

    load = jnp.concatenate([mix[0], t_stat], axis=0)
    part = spread(load, "z").reshape(8 * 80, LANE)
    last = spread(part, ("xh", "y", "xl")).reshape(2, 64, 80, LANE)
    last_rows = last[:, :, :HALF]
    last_stat = last[:, :, HALF:].reshape(128, 16, LANE)

    n_last, logits, probs, stat = call(
        logits_kernel,
        (
            sds((64, TOK, LANE), BF16),
            sds((STEPS, LANE, TOK), F32),
            sds((STEPS, LANE, TOK), BF16),
            sds((8, 16, LANE), F32),
        ),
        (SMEM, SMEM) + (VMEM,) * 9,
        flops=6 * 128 * 8192 * 128,
        nbytes=10 << 20,
        scratch=[pltpu.VMEM((TOK, LANE), F32)],
    )(
        pos,
        shifts,
        last_rows,
        last_stat,
        draft_gain,
        draft_head,
        mine[0],
        theirs[0],
        mine[1],
        theirs[1],
        t_logits,
    )

    def from_other(values):
        rows = values.shape[1]
        half = lax.dynamic_slice(values, ((1 - c) * 32, 0, 0), (32, rows, LANE))
        return swap(half, "c")

    across = [from_other(v) for v in (mine[0], theirs[0], mine[1], theirs[1], n_last)]

    stat = lax.all_to_all(stat, "z", 0, 0, tiled=True)
    stat = call(middle_kernel, sds((16, 16, LANE), F32), (VMEM,))(stat)
    stat = lax.all_to_all(stat, ("xh", "y", "xl"), 0, 0, tiled=True)

    mask = lax.dynamic_slice_in_dim(loss_mask, c * TOK, TOK, 0).astype(F32)[None, :]
    grads, kl = call(
        functools.partial(grad_kernel, vocab_total),
        (sds((STEPS, LANE, TOK), BF16), sds((8, LANE), F32)),
        (SMEM,) + (VMEM,) * 4,
    )(pos, stat, mask, logits, probs)
    grads_got, kl_got = swap(grads, "c"), swap(kl, "c")

    head_grad = call(
        head_kernel,
        sds((32, LANE, LANE), BF16),
        (SMEM,) + (VMEM,) * 12,
        flops=2 * 768 * 4096 * 128,
        nbytes=8 << 20,
    )(
        pos,
        grads,
        grads_got,
        mine[0],
        theirs[0],
        mine[1],
        theirs[1],
        n_last,
        *across,
    ).reshape(4096, LANE)

    blocks = TOK // BLK
    kl_own, kl_other = kl[:STEPS], kl_got[:STEPS]
    kl_all = jnp.where(c == 0, jnp.stack([kl_own, kl_other], 1), jnp.stack([kl_other, kl_own], 1))
    kl_all = kl_all.reshape(STEPS, 2, 1, blocks, BLK)
    hits = (owner[:, 0].reshape(2, blocks) == c).astype(jnp.int32)
    rank = jnp.cumsum(hits, axis=1) - 1
    pick = (hits[:, None, :] > 0) & (
        rank[:, None, :] == jnp.arange(MOST, dtype=jnp.int32)[None, :, None]
    )
    slot_kl = jnp.sum(jnp.where(pick[None, :, :, :, None], kl_all, 0.0), axis=3)
    return head_grad, slot_kl.reshape(STEPS, 2 * MOST * BLK)


def solution(mesh):
    fine = Mesh(np.asarray(mesh.devices).reshape(2, 4, 2, 8, 2), ("xh", "y", "xl", "z", "c"))
    tp = ("y", "xl", "z")
    every = ("xh",) + tp
    return jax.shard_map(
        on_device,
        mesh=fine,
        in_specs=(
            P("c", None, tp),
            P(),
            P(),
            P(),
            P(),
            P(),
            P(None, every),
            P("xh", tp),
            P("xh", tp),
            P(),
            P(None, tp),
            P(None, every),
        ),
        out_specs=(P("c", every), P(None, "c")),
        check_vma=False,
    )
```

time: 2380 us -> 342 us (0.14)
  waiting for transfers between devices: 1220 us -> 146 us
  blocking collectives: 1050 us -> 77.5 us
  starting transfers between devices: 0.48 us -> 54.7 us
  matrix products: 30.9 us -> 0 us
  other arithmetic: 32.8 us -> 5.33 us
  Pallas kernels: 0 us -> 26 us
    all_gather x5 -> x0, waiting for transfers between devices: 1120 us -> none  [width_rows(): return lax.all_gather(values, 'tp', axis=1, tiled=True)]
    psum x3 -> x0, blocking collectives: 596 us -> none  [the longest x2 584 us: vocab_totals(): summed = lax.psum((totals, extra_one, extra_two), ('grp', 'tp'))]
    pmax x1 -> x0, blocking collectives: 292 us -> none  [vocab_totals(): peak_val = lax.pmax(local_peak, ('grp', 'tp'))]
    all_to_all x2 -> x5, blocking collectives: 158 us -> 77.5 us  [the longest x3 49.5 us: spread(): lax.all_to_all(jnp.broadcast_to(values[None], (count,) + values.shape), a...]
    all_to_all x0 -> x5, waiting for transfers between devices: none -> 78.5 us  [the longest x3 70.7 us: spread(): lax.all_to_all(jnp.broadcast_to(values[None], (count,) + values.shape), a...]
    ppermute x0 -> x13, waiting for transfers between devices: none -> 67.2 us  [the longest x12 67.2 us: swap(): lax.ppermute(values, axis, [(i, (i + count // 2) % count) for i in range(...]
    reduce_scatter x1 -> x0, waiting for transfers between devices: 63.4 us -> none  [on_device(): lax.psum_scatter(total_grad, 'seq', scatter_dimension=0, tiled=True)]
    psum x1 -> x0, waiting for transfers between devices: 34.5 us -> none  [group_sums(): return lax.psum((united_part, embed_part), 'grp')]
  transfers between devices with their start and end apart: 7 -> 18, of which waited for: 7 -> 10; matrix products, arithmetic and copies ran while one was open for 1% -> 5% of each run, Pallas kernels for 0% -> 3%
where the time goes in v1:
time: 342 us; the launch traced here: 341 us
  waiting for transfers between devices  146 us (43%)
  blocking collectives  77.5 us (23%)
  starting transfers between devices  54.7 us (16%)
  local copies, waits for them, and re-layouts  30.7 us (9%)
  Pallas kernels  26 us (8%)
  other arithmetic  5.33 us (2%)
    all_to_all x3, waiting for transfers between devices, spread(): lax.all_to_all(jnp.broadcast_to(values[None], (count,) + values.shape), a...  70.7 us
    ppermute x12, waiting for transfers between devices, swap(): lax.ppermute(values, axis, [(i, (i + count // 2) % count) for i in range(...  67.2 us
    all_to_all x3, blocking collectives, spread(): lax.all_to_all(jnp.broadcast_to(values[None], (count,) + values.shape), a...  49.5 us
    ppermute x12, starting transfers between devices, swap(): lax.ppermute(values, axis, [(i, (i + count // 2) % count) for i in range(...  28.4 us
    all_to_all x2, blocking collectives, on_device(): part = lax.all_to_all(mix, 'z', 0, 0, tiled=True).reshape(8 * HALF, LANE)  28 us
    all_to_all x3, starting transfers between devices, spread(): lax.all_to_all(jnp.broadcast_to(values[None], (count,) + values.shape), a...  14.1 us
    dynamic_slice x5, local copies, waits for them, and re-layouts, from_other(): half = lax.dynamic_slice(values, ((1 - c) * 32, 0, 0), (32, rows, LANE))  8.88 us
    pallas_call x1, Pallas kernels, on_device(): call(head_kernel, sds((32, LANE, LANE), BF16), (SMEM,) + (VMEM,) * 12, fl...  7.58 us
  transfers between devices with their start and end apart: 18, of which 10 were waited for; matrix products, arithmetic and copies ran while one was open for 5% of the time, Pallas kernels for 3%

profile of v1, /device:TPU:1, one launch (start us, length us, event | category | flops | bytes accessed | tf_op | source)
XLA Modules:
  0.0 340.7 jit_solution(8501207196363900470)
XLA Ops:
  1.6 3.8 %collective-permute-start = (bf16[64,128]{1,0:T(8,128)(2,1)S(1)}, bf16[64,128]{1,0:T(8,128)(2,1)S(1)}, u32[]{:S(2)}, u32[]{:S(2)}) collective-permute-start(bf16[64,128]{1,0:T(8,128)(2,1)S(1)} %dynamic-slice_bitcast_fusion.2), channel_id=1, source_target_pairs={{0,64},{32,96},{64,0},{96,32},{1,65},{33,97},{65,1},{97,33},{2,66}... | collective-permute-start | bytes 49160 | tf_op jit(solution)/shard_map/ppermute | solution.py:55
  6.7 19.7 %all_to_all.50 = bf16[8,192,128]{2,1,0:T(8,128)(2,1)S(1)} all-to-all(bf16[8,192,128]{2,1,0:T(8,128)(2,1)S(1)} %broadcast_in_dim.96), channel_id=1, replica_groups=mesh['xh'=2,'y'=4,'xl'=2,'z'=8,'c'=2] {'z'}, dimensions={0} | all-to-all | bytes 786432 | tf_op jit(solution)/shard_map/all_to_all | solution.py:48
  28.4 5.2 %all-to-all-start.1 = ((bf16[8,1536,128]{2,1,0:T(8,128)(2,1)}), bf16[8,1536,128]{2,1,0:T(8,128)(2,1)}, u32[]{:S(2)}, u32[]{:S(2)}) async-start(bf16[8,1536,128]{2,1,0:T(8,128)(2,1)} %broadcast_in_dim.98), calls=%async_computation.1 | async-start | bytes 6291456 | tf_op jit(solution)/shard_map/all_to_all | solution.py:48
  34.8 32.6 %all-to-all-done.1 = bf16[8,1536,128]{2,1,0:T(8,128)(2,1)} async-done(((bf16[8,1536,128]{2,1,0:T(8,128)(2,1)}), bf16[8,1536,128]{2,1,0:T(8,128)(2,1)}, u32[]{:S(2)}, u32[]{:S(2)}) %all-to-all-start.1) | async-done | bytes 3145760 | tf_op jit(solution)/shard_map/all_to_all | solution.py:48
  71.9 4.0 %shard_map.131 = (f32[64,128]{1,0:T(8,128)S(1)}, f32[64,128]{1,0:T(8,128)S(1)}) custom-call(s32[2]{0:T(128)S(1)} %pad_add_fusion.pos_ref, bf16[64,192,128]{2,1,0:T(8,128)(2,1)} %bitcast.7.x_ref, bf16[12288,128]{1,0:T(8,128)(2,1)} %fc_ref.1), custom_call_target="tpu_custom_call" | custom-call | flops 402653184 | bytes 6291456 | tf_op jit(solution)/shard_map/pallas_call | solution.py:326
  75.9 5.0 %collective-permute-start.1 = (f32[64,128]{1,0:T(8,128)S(1)}, f32[64,128]{1,0:T(8,128)S(1)}, u32[]{:S(2)}, u32[]{:S(2)}) collective-permute-start(f32[64,128]{1,0:T(8,128)S(1)} %get-tuple-element.21), channel_id=1, source_target_pairs={{0,128},{128,0},{1,129},{129,1},{2,130},{130,2},{3,131},{131,3},{4... | collective-permute-start | bytes 98312 | tf_op jit(solution)/shard_map/ppermute | solution.py:55
  81.1 35.9 %collective-permute-done.2.e_got_ref = bf16[64,128]{1,0:T(8,128)(2,1)S(1)} collective-permute-done((bf16[64,128]{1,0:T(8,128)(2,1)S(1)}, bf16[64,128]{1,0:T(8,128)(2,1)S(1)}, u32[]{:S(2)}, u32[]{:S(2)}) %collective-permute-start.2) | collective-permute-done | bytes 16416 | tf_op jit(solution)/shard_map/ppermute | solution.py:55
  117.7 17.7 %all_to_all.51 = bf16[8,64,128]{2,1,0:T(8,128)(2,1)S(1)} all-to-all(bf16[8,64,128]{2,1,0:T(8,128)(2,1)S(1)} %get-tuple-element.22), channel_id=1, replica_groups=mesh['xh'=2,'y'=4,'xl'=2,'z'=8,'c'=2] {'z'}, dimensions={0} | all-to-all | bytes 262144 | tf_op jit(solution)/shard_map/all_to_all | solution.py:347
  135.5 19.2 %all_to_all.52 = bf16[8,512,128]{2,1,0:T(8,128)(2,1)S(1)} all-to-all(bf16[8,512,128]{2,1,0:T(8,128)(2,1)S(1)} %broadcast_in_dim.107), channel_id=1, replica_groups=mesh['xh'=2,'y'=4,'xl'=2,'z'=8,'c'=2] {'y','xl'}, dimensions={0} | all-to-all | bytes 2097152 | tf_op jit(solution)/shard_map/all_to_all | solution.py:48
  156.0 10.3 %all_to_all.53 = bf16[8,64,128]{2,1,0:T(8,128)(2,1)S(1)} all-to-all(bf16[8,64,128]{2,1,0:T(8,128)(2,1)S(1)} %get-tuple-element.25), channel_id=1, replica_groups=mesh['xh'=2,'y'=4,'xl'=2,'z'=8,'c'=2] {'z'}, dimensions={0} | all-to-all | bytes 262144 | tf_op jit(solution)/shard_map/all_to_all | solution.py:347
  167.4 4.2 %all-to-all-start.5 = ((bf16[8,512,128]{2,1,0:T(8,128)(2,1)}), bf16[8,512,128]{2,1,0:T(8,128)(2,1)}, u32[]{:S(2)}, u32[]{:S(2)}) async-start(bf16[8,512,128]{2,1,0:T(8,128)(2,1)} %broadcast_in_dim.109), calls=%async_computation.5 | async-start | bytes 2097152 | tf_op jit(solution)/shard_map/all_to_all | solution.py:48
  175.7 6.5 %all-to-all-done.5 = bf16[8,512,128]{2,1,0:T(8,128)(2,1)} async-done(((bf16[8,512,128]{2,1,0:T(8,128)(2,1)}), bf16[8,512,128]{2,1,0:T(8,128)(2,1)}, u32[]{:S(2)}, u32[]{:S(2)}) %all-to-all-start.5) | async-done | bytes 1048608 | tf_op jit(solution)/shard_map/all_to_all | solution.py:48
  187.4 10.7 %all_to_all.54 = bf16[8,80,128]{2,1,0:T(8,128)(2,1)S(1)} all-to-all(bf16[8,80,128]{2,1,0:T(8,128)(2,1)S(1)} %broadcast_in_dim.110), channel_id=1, replica_groups=mesh['xh'=2,'y'=4,'xl'=2,'z'=8,'c'=2] {'z'}, dimensions={0} | all-to-all | bytes 327680 | tf_op jit(solution)/shard_map/all_to_all | solution.py:48
  200.1 4.6 %all-to-all-start.7 = ((bf16[16,640,128]{2,1,0:T(8,128)(2,1)}), bf16[16,640,128]{2,1,0:T(8,128)(2,1)}, u32[]{:S(2)}, u32[]{:S(2)}) async-start(bf16[16,640,128]{2,1,0:T(8,128)(2,1)} %broadcast_in_dim.112), calls=%async_computation.7 | async-start | bytes 5242880 | tf_op jit(solution)/shard_map/all_to_all | solution.py:48
  209.2 31.5 %all-to-all-done.7 = bf16[16,640,128]{2,1,0:T(8,128)(2,1)} async-done(((bf16[16,640,128]{2,1,0:T(8,128)(2,1)}), bf16[16,640,128]{2,1,0:T(8,128)(2,1)}, u32[]{:S(2)}, u32[]{:S(2)}) %all-to-all-start.7) | async-done | bytes 2621472 | tf_op jit(solution)/shard_map/all_to_all | solution.py:48
  240.7 3.2 slice.35.x_ref
  245.0 6.9 %collective-permute-done.4.b0_ref = bf16[64,64,128]{2,1,0:T(8,128)(2,1)} collective-permute-done((bf16[64,64,128]{2,1,0:T(8,128)(2,1)S(1)}, bf16[64,64,128]{2,1,0:T(8,128)(2,1)}, u32[]{:S(2)}, u32[]{:S(2)}) %collective-permute-start.4) | collective-permute-done | bytes 1048608 | tf_op jit(solution)/shard_map/ppermute | solution.py:55
  252.0 22.5 %collective-permute-done.5.b1_ref = bf16[64,64,128]{2,1,0:T(8,128)(2,1)} collective-permute-done((bf16[64,64,128]{2,1,0:T(8,128)(2,1)}, bf16[64,64,128]{2,1,0:T(8,128)(2,1)}, u32[]{:S(2)}, u32[]{:S(2)}) %collective-permute-start.5) | collective-permute-done | bytes 1048608 | tf_op jit(solution)/shard_map/ppermute | solution.py:55
  274.4 7.2 %shard_map.136 = (bf16[64,128,128]{2,1,0:T(8,128)(2,1)}, f32[3,128,128]{2,1,0:T(8,128)S(1)}, bf16[3,128,128]{2,1,0:T(8,128)(2,1)S(1)}, f32[8,16,128]{2,1,0:T(8,128)S(1)}) custom-call(s32[2]{0:T(128)S(1)} %pad_add_fusion.pos_ref, s32[3]{0:T(128)S(1)} %copy-done.17, bf16[2,64,64,128]{3,2,1,0:T(8,128)(2,1)} %slice.35.x_ref, bf16[128,16,128]{2,1,0:T(8,128)(2,1)S(1)} %bitcast.30, ...), custom_call_target="tpu_custom_call" | custom-call | flops 805306368 | bytes 10485760 | tf_op jit(solution)/shard_map/pallas_call | solution.py:379
  284.0 10.4 %collective-permute-start.11 = (bf16[32,128,128]{2,1,0:T(8,128)(2,1)}, bf16[32,128,128]{2,1,0:T(8,128)(2,1)}, u32[]{:S(2)}, u32[]{:S(2)}) collective-permute-start(bf16[32,128,128]{2,1,0:T(8,128)(2,1)} %constant_dynamic-slice_fusion), channel_id=1, source_target_pairs={{0,1},{1,0},{2,3},{3,2},{4,5},{5,4},{6,7},{7,6},{8,9},{9,8},{10,11... | collective-permute-start | bytes 3145736 | tf_op jit(solution)/shard_map/ppermute | solution.py:55
  295.2 3.4 all-to-all-start.8
  301.0 4.8 %all-to-all-done.8.in_ref = f32[8,16,128]{2,1,0:T(8,128)S(1)} async-done(((f32[8,16,128]{2,1,0:T(8,128)}), f32[8,16,128]{2,1,0:T(8,128)S(1)}, u32[]{:S(2)}, u32[]{:S(2)}) %all-to-all-start.8) | async-done | bytes 65568 | tf_op jit(solution)/shard_map/all_to_all | solution.py:412
  306.5 7.6 %all-to-all-start.9 = ((f32[16,16,128]{2,1,0:T(8,128)}), f32[16,16,128]{2,1,0:T(8,128)S(1)}, u32[]{:S(2)}, u32[]{:S(2)}) async-start(f32[16,16,128]{2,1,0:T(8,128)} %shard_map.137), calls=%async_computation.9 | async-start | bytes 262144 | tf_op jit(solution)/shard_map/all_to_all | solution.py:414
  333.1 7.6 %shard_map.139 = bf16[32,128,128]{2,1,0:T(8,128)(2,1)} custom-call(s32[2]{0:T(128)S(1)} %copy-done.16, bf16[3,128,128]{2,1,0:T(8,128)(2,1)S(1)} %copy-done.9, bf16[3,128,128]{2,1,0:T(8,128)(2,1)S(1)} %collective-permute-done.6.h_ref, bf16[64,64,128]{2,1,0:T(8,128)(2,1)S(1)} %get-tuple-element.29.a0_ref, bf16[64,64,128]{2,1,0:T(8,128)(2,1)} %collective-permute-done.4.b0_ref, ...), custom_call_target="tpu_custom_call" | custom-call | flops 805306368 | bytes 8388608 | tf_op jit(solution)/shard_map/pallas_call | solution.py:424
  (117 shorter events, 55.4 us)
Async XLA Ops:
  1.6 5.0 %collective-permute-start = (bf16[64,128]{1,0:T(8,128)(2,1)S(1)}, bf16[64,128]{1,0:T(8,128)(2,1)S(1)}, u32[]{:S(2)}, u32[]{:S(2)}) collective-permute-start(bf16[64,128]{1,0:T(8,128)(2,1)S(1)} %dynamic-slice_bitcast_fusion.2), channel_id=1, source_target_pairs={{0,64},{32,96},{64,0},{96,32},{1,65},{33,97},{65,1},{97,33},{2,66}... | collective-permute-start | bytes 49160 | tf_op jit(solution)/shard_map/ppermute | solution.py:55
  28.4 39.0 %all-to-all-start.1 = ((bf16[8,1536,128]{2,1,0:T(8,128)(2,1)}), bf16[8,1536,128]{2,1,0:T(8,128)(2,1)}, u32[]{:S(2)}, u32[]{:S(2)}) async-start(bf16[8,1536,128]{2,1,0:T(8,128)(2,1)} %broadcast_in_dim.98), calls=%async_computation.1 | async-start | bytes 6291456 | tf_op jit(solution)/shard_map/all_to_all | solution.py:48
  70.6 101.1 %collective-permute-start.3 = (bf16[64,128,128]{2,1,0:T(8,128)(2,1)}, bf16[64,128,128]{2,1,0:T(8,128)(2,1)}, u32[]{:S(2)}, u32[]{:S(2)}) collective-permute-start(bf16[64,128,128]{2,1,0:T(8,128)(2,1)} %slice.34), channel_id=1, source_target_pairs={{128,0},{129,1},{130,2},{131,3},{132,4},{133,5},{134,6},{135,7},{1... | collective-permute-start | bytes 6291464 | tf_op jit(solution)/shard_map/ppermute | solution.py:337
  71.9 202.5 %copy-start.14 = (s32[2]{0:T(128)}, s32[2]{0:T(128)S(1)}, u32[]{:S(2)}) copy-start(s32[2]{0:T(128)S(1)} %pad_add_fusion.pos_ref) | copy-start | bytes 28
  71.9 45.0 %copy-start.17 = (s32[3]{0:T(128)S(1)}, s32[3]{0:T(128)}, u32[]{:S(2)}) copy-start(s32[3]{0:T(128)} %shifts_ref.7) | copy-start | bytes 40
  75.9 78.8 %copy-start.1 = (bf16[8192,128]{1,0:T(8,128)(2,1)S(1)}, bf16[8192,128]{1,0:T(8,128)(2,1)}, u32[]{:S(2)}) copy-start(bf16[8192,128]{1,0:T(8,128)(2,1)} %w_ref.5) | copy-start | bytes 6291460
  75.9 78.8 %copy-start.7 = (bf16[8192]{0:T(1024)(128)(2,1)S(1)}, bf16[8192]{0:T(1024)(128)(2,1)}, u32[]{:S(2)}) copy-start(bf16[8192]{0:T(1024)(128)(2,1)} %param.21) | copy-start | bytes 49156
  75.9 41.0 %collective-permute-start.1 = (f32[64,128]{1,0:T(8,128)S(1)}, f32[64,128]{1,0:T(8,128)S(1)}, u32[]{:S(2)}, u32[]{:S(2)}) collective-permute-start(f32[64,128]{1,0:T(8,128)S(1)} %get-tuple-element.21), channel_id=1, source_target_pairs={{0,128},{128,0},{1,129},{129,1},{2,130},{130,2},{3,131},{131,3},{4... | collective-permute-start | bytes 98312 | tf_op jit(solution)/shard_map/ppermute | solution.py:55
  80.9 36.0 %collective-permute-start.2 = (bf16[64,128]{1,0:T(8,128)(2,1)S(1)}, bf16[64,128]{1,0:T(8,128)(2,1)S(1)}, u32[]{:S(2)}, u32[]{:S(2)}) collective-permute-start(bf16[64,128]{1,0:T(8,128)(2,1)S(1)} %get-tuple-element.42), channel_id=1, source_target_pairs={{0,128},{128,0},{1,129},{129,1},{2,130},{130,2},{3,131},{131,3},{4... | collective-permute-start | bytes 49160 | tf_op jit(solution)/shard_map/ppermute | solution.py:55
  167.4 14.8 %all-to-all-start.5 = ((bf16[8,512,128]{2,1,0:T(8,128)(2,1)}), bf16[8,512,128]{2,1,0:T(8,128)(2,1)}, u32[]{:S(2)}, u32[]{:S(2)}) async-start(bf16[8,512,128]{2,1,0:T(8,128)(2,1)} %broadcast_in_dim.109), calls=%async_computation.5 | async-start | bytes 2097152 | tf_op jit(solution)/shard_map/all_to_all | solution.py:48
  200.1 40.6 %all-to-all-start.7 = ((bf16[16,640,128]{2,1,0:T(8,128)(2,1)}), bf16[16,640,128]{2,1,0:T(8,128)(2,1)}, u32[]{:S(2)}, u32[]{:S(2)}) async-start(bf16[16,640,128]{2,1,0:T(8,128)(2,1)} %broadcast_in_dim.112), calls=%async_computation.7 | async-start | bytes 5242880 | tf_op jit(solution)/shard_map/all_to_all | solution.py:48
  204.7 47.3 %collective-permute-start.4 = (bf16[64,64,128]{2,1,0:T(8,128)(2,1)S(1)}, bf16[64,64,128]{2,1,0:T(8,128)(2,1)}, u32[]{:S(2)}, u32[]{:S(2)}) collective-permute-start(bf16[64,64,128]{2,1,0:T(8,128)(2,1)S(1)} %get-tuple-element.29.a0_ref), channel_id=1, source_target_pairs={{0,128},{128,0},{1,129},{129,1},{2,130},{130,2},{3,131},{131,3},{4... | collective-permute-start | bytes 3145736 | tf_op jit(solution)/shard_map/ppermute | solution.py:55
  207.4 67.0 %collective-permute-start.5 = (bf16[64,64,128]{2,1,0:T(8,128)(2,1)}, bf16[64,64,128]{2,1,0:T(8,128)(2,1)}, u32[]{:S(2)}, u32[]{:S(2)}) collective-permute-start(bf16[64,64,128]{2,1,0:T(8,128)(2,1)} %copy-done.3), channel_id=1, source_target_pairs={{0,128},{128,0},{1,129},{129,1},{2,130},{130,2},{3,131},{131,3},{4... | collective-permute-start | bytes 3145736 | tf_op jit(solution)/shard_map/ppermute | solution.py:55
  284.0 36.9 %copy-start.15 = (s32[2]{0:T(128)S(1)}, s32[2]{0:T(128)}, u32[]{:S(2)}) copy-start(s32[2]{0:T(128)} %copy-done.14) | copy-start | bytes 28
  284.0 36.9 %copy-start.18 = (f32[1,128]{1,0:T(1,128)S(1)}, f32[1,128]{1,0:T(1,128)}, u32[]{:S(2)}) copy-start(f32[1,128]{1,0:T(1,128)} %convert_bitcast_fusion.mask_ref) | copy-start | bytes 1540
  284.0 46.4 %collective-permute-start.11 = (bf16[32,128,128]{2,1,0:T(8,128)(2,1)}, bf16[32,128,128]{2,1,0:T(8,128)(2,1)}, u32[]{:S(2)}, u32[]{:S(2)}) collective-permute-start(bf16[32,128,128]{2,1,0:T(8,128)(2,1)} %constant_dynamic-slice_fusion), channel_id=1, source_target_pairs={{0,1},{1,0},{2,3},{3,2},{4,5},{5,4},{6,7},{7,6},{8,9},{9,8},{10,11... | collective-permute-start | bytes 3145736 | tf_op jit(solution)/shard_map/ppermute | solution.py:55
  295.2 33.1 %collective-permute-start.7 = (bf16[32,64,128]{2,1,0:T(8,128)(2,1)}, bf16[32,64,128]{2,1,0:T(8,128)(2,1)}, u32[]{:S(2)}, u32[]{:S(2)}) collective-permute-start(bf16[32,64,128]{2,1,0:T(8,128)(2,1)} %constant_dynamic-slice_fusion.4), channel_id=1, source_target_pairs={{0,1},{1,0},{2,3},{3,2},{4,5},{5,4},{6,7},{7,6},{8,9},{9,8},{10,11... | collective-permute-start | bytes 1572872 | tf_op jit(solution)/shard_map/ppermute | solution.py:55
  295.2 10.5 %all-to-all-start.8 = ((f32[8,16,128]{2,1,0:T(8,128)}), f32[8,16,128]{2,1,0:T(8,128)S(1)}, u32[]{:S(2)}, u32[]{:S(2)}) async-start(f32[8,16,128]{2,1,0:T(8,128)} %copy-done.12), calls=%async_computation.8 | async-start | bytes 131072 | tf_op jit(solution)/shard_map/all_to_all | solution.py:412
  300.5 29.2 %collective-permute-start.8 = (bf16[32,64,128]{2,1,0:T(8,128)(2,1)}, bf16[32,64,128]{2,1,0:T(8,128)(2,1)}, u32[]{:S(2)}, u32[]{:S(2)}) collective-permute-start(bf16[32,64,128]{2,1,0:T(8,128)(2,1)} %constant_dynamic-slice_fusion.3), channel_id=1, source_target_pairs={{0,1},{1,0},{2,3},{3,2},{4,5},{5,4},{6,7},{7,6},{8,9},{9,8},{10,11... | collective-permute-start | bytes 1572872 | tf_op jit(solution)/shard_map/ppermute | solution.py:55
  306.5 14.4 %all-to-all-start.9 = ((f32[16,16,128]{2,1,0:T(8,128)}), f32[16,16,128]{2,1,0:T(8,128)S(1)}, u32[]{:S(2)}, u32[]{:S(2)}) async-start(f32[16,16,128]{2,1,0:T(8,128)} %shard_map.137), calls=%async_computation.9 | async-start | bytes 262144 | tf_op jit(solution)/shard_map/all_to_all | solution.py:414
  316.0 13.7 %collective-permute-start.9 = (bf16[32,64,128]{2,1,0:T(8,128)(2,1)}, bf16[32,64,128]{2,1,0:T(8,128)(2,1)}, u32[]{:S(2)}, u32[]{:S(2)}) collective-permute-start(bf16[32,64,128]{2,1,0:T(8,128)(2,1)} %constant_dynamic-slice_fusion.2), channel_id=1, source_target_pairs={{0,1},{1,0},{2,3},{3,2},{4,5},{5,4},{6,7},{7,6},{8,9},{9,8},{10,11... | collective-permute-start | bytes 1572872 | tf_op jit(solution)/shard_map/ppermute | solution.py:55
  323.2 4.9 %collective-permute-start.12 = (f32[8,128]{1,0:T(8,128)S(1)}, f32[8,128]{1,0:T(8,128)S(1)}, u32[]{:S(2)}, u32[]{:S(2)}) collective-permute-start(f32[8,128]{1,0:T(8,128)S(1)} %get-tuple-element.37), channel_id=1, source_target_pairs={{0,1},{1,0},{2,3},{3,2},{4,5},{5,4},{6,7},{7,6},{8,9},{9,8},{10,11... | collective-permute-start | bytes 12296 | tf_op jit(solution)/shard_map/ppermute | solution.py:55
  328.1 2.3 collective-permute-start.10
  328.3 2.0 collective-permute-start.6
  (19 other events, 229.5 us)

commit v2 on v1

v2 whole, which is shorter than its diff:
```python
import functools

import jax
import jax.numpy as jnp
import numpy as np
from jax import lax
from jax.experimental import pallas as pl
from jax.experimental.pallas import tpu as pltpu
from jax.sharding import Mesh
from jax.sharding import PartitionSpec as P

BLK = 16
STEPS = 3
MOST = 6
LANE = 128
HALF = 64
TOK = 128
EPS = 1e-05

VMEM = pl.BlockSpec(memory_space=pltpu.VMEM)
SMEM = pl.BlockSpec(memory_space=pltpu.SMEM)
ANY = pl.BlockSpec(memory_space=pl.ANY)
F32 = jnp.float32
BF16 = jnp.bfloat16


def call(kernel, outs, ins, *, flops=0, nbytes=0, scratch=(), sems=0, far=(), big=True):
    return pl.pallas_call(
        kernel,
        out_shape=tuple(outs),
        in_specs=list(ins),
        out_specs=tuple(ANY if i in far else VMEM for i in range(len(outs))),
        scratch_shapes=list(scratch) + ([pltpu.SemaphoreType.DMA((sems,))] if sems else []),
        compiler_params=pltpu.CompilerParams(vmem_limit_bytes=(60 if big else 4) * 1024 * 1024),
        cost_estimate=pl.CostEstimate(flops=flops, bytes_accessed=nbytes, transcendentals=0),
    )


def sds(shape, dtype):
    return jax.ShapeDtypeStruct(shape, dtype)


def begin(source, target, sem):
    copy = pltpu.make_async_copy(source, target, sem)
    copy.start()
    return copy


def dot(a, b):
    return jnp.dot(a, b, preferred_element_type=F32)


def spread(values, axis):
    count = lax.axis_size(axis)
    return lax.all_to_all(
        jnp.broadcast_to(values[None], (count,) + values.shape), axis, 0, 0, tiled=True
    )


def across_grp(values, pairs=((0, 3), (1, 2), (2, 1), (3, 0))):
    return lax.ppermute(values, ("xh", "xl"), list(pairs))


def swap(values, axis):
    count = lax.axis_size(axis)
    return lax.ppermute(values, axis, [(i, (i + count // 2) % count) for i in range(count)])


def shift_lanes(values, shift):
    place = lax.broadcasted_iota(jnp.int32, values.shape, 1) & (BLK - 1)
    ahead = pltpu.roll(values, (TOK - shift) & (TOK - 1), 1)
    return jnp.where(place + shift < BLK, ahead, pltpu.roll(values, BLK - shift, 1))


def shift_rows(shift, rows):
    tok = lax.broadcasted_iota(jnp.int32, (rows, rows), 0)
    src = lax.broadcasted_iota(jnp.int32, (rows, rows), 1)
    want = (tok & ~(BLK - 1)) + ((tok & (BLK - 1)) + shift & (BLK - 1))
    return jnp.where(src == want, 1.0, 0.0).astype(BF16)


def unite_kernel(pos_ref, a_ref, *rest):
    ring, (fc_ref, own_ref, other_ref, x_ref, w_ref, m_ref, v_ref, acc_ref, sem) = rest[:9], rest[9:]
    g, z = pos_ref[0], pos_ref[2]
    whole = pl.multiple_of(g * 4096, 4096)
    middle = pl.multiple_of((1 - g) * 8192, 4096)
    first = []
    for i in range(4):
        rows = pl.ds(whole + i * 2048, 2048)
        first.append(begin(a_ref.at[pl.ds(i * 16, 16)], x_ref.at[pl.ds(i * 16, 16)], sem.at[2 * i]))
        first.append(begin(fc_ref.at[rows], w_ref.at[pl.ds(i * 2048, 2048)], sem.at[2 * i + 1]))
    second = [begin(fc_ref.at[pl.ds(middle, 4096)], v_ref, sem.at[8])]
    for n, (ref, away) in enumerate(zip(ring[:7], (0, -1, 1, -2, 2, -3, 3))):
        second.append(begin(ref, m_ref.at[(z + away + 8) & 7], sem.at[9 + n]))
    second.append(begin(ring[7], m_ref.at[(z + 4) & 7, pl.ds(0, 1)], sem.at[16]))
    second.append(begin(ring[8], m_ref.at[(z + 4) & 7, pl.ds(1, 1)], sem.at[17]))
    acc = jnp.zeros((TOK, LANE), F32)
    for i in range(4):
        first[2 * i].wait()
        first[2 * i + 1].wait()
        lhs = jnp.concatenate([x_ref[i * 16 + j] for j in range(16)], axis=1)
        acc += dot(lhs, w_ref[i * 2048 : (i + 1) * 2048, :])
    for copy in second:
        copy.wait()
    for yl in range(2):
        for xl in range(2):
            lhs = jnp.concatenate([m_ref[j, xl, yl] for j in range(8)], axis=1)
            at = (yl * 2 + xl) * 1024
            acc += dot(lhs, v_ref[at : at + 1024, :])
    acc_ref[...] = acc
    own_ref[...] = acc_ref[pl.ds(pl.multiple_of(g * HALF, HALF), HALF), :]
    other_ref[...] = acc_ref[pl.ds(pl.multiple_of((1 - g) * HALF, HALF), HALF), :]


def first_kernel(shifts_ref, own_ref, got_ref, e_own_ref, e_got_ref, state_ref, e_ref, mix_ref):
    state = (own_ref[...] + got_ref[...]).astype(BF16).astype(F32)
    state_ref[...] = state
    rows = (e_own_ref[...].astype(F32) + e_got_ref[...].astype(F32)).astype(BF16)
    e_ref[...] = rows
    mixed = (state + dot(shift_rows(shifts_ref[0], HALF), rows)).astype(BF16)
    for i in range(64):
        mix_ref[i] = mixed


def normalize_into(x_of, gain_ref, count, rows, out_of, ready=None):
    total = jnp.zeros((rows, LANE), F32)
    for p in range(count):
        if ready is not None and p % 16 == 0:
            for copy in ready[p // 16]:
                copy.wait()
        v = x_of(p).astype(F32)
        total += v * v
    scale = lax.rsqrt(jnp.sum(total, axis=1, keepdims=True) / (count * LANE) + EPS)
    for i in range(count // 16):
        gain = gain_ref[i].astype(F32)
        for j in range(16):
            p = i * 16 + j
            out_of(p, (x_of(p).astype(F32) * scale * gain[j : j + 1, :]).astype(BF16))


def row_dot(n_of, w_ref, rows):
    acc = jnp.zeros((rows, LANE), F32)
    for i in range(4):
        lhs = jnp.concatenate([n_of(i * 16 + j) for j in range(16)], axis=1)
        acc += dot(lhs, w_ref[i * 2048 : (i + 1) * 2048, :])
    return acc


def layer_kernel(
    step,
    pos_ref,
    shifts_ref,
    far_x_ref,
    gain_ref,
    far_w_ref,
    state_ref,
    e_ref,
    low_ref,
    high_ref,
    half_ref,
    next_ref,
    mix_ref,
    x_ref,
    w_ref,
    n_ref,
    sem,
):
    ready = []
    for i in range(4):
        part = pl.ds(i * 16, 16)
        ready.append([begin(far_x_ref.at[part], x_ref.at[part], sem.at[i])])
    weights = begin(far_w_ref, w_ref, sem.at[4])

    def put(p, value):
        n_ref[p] = value

    normalize_into(lambda p: x_ref[p], gain_ref, 64, HALF, put, ready)
    low = begin(n_ref.at[pl.ds(0, 32)], low_ref, sem.at[5])
    high = begin(n_ref.at[pl.ds(32, 32)], high_ref, sem.at[7])
    half = begin(n_ref.at[pl.ds((1 - pos_ref[1]) * 32, 32)], half_ref, sem.at[6])
    weights.wait()
    acc = row_dot(lambda p: n_ref[p], w_ref, HALF)
    state = state_ref[...] + acc * jax.nn.sigmoid(acc)
    next_ref[...] = state
    mixed = (state + dot(shift_rows(shifts_ref[step + 1], HALF), e_ref[...])).astype(BF16)
    if step == 0:
        for i in range(64):
            mix_ref[i] = mixed
    else:
        for i in range(8):
            mix_ref[i] = mixed
    low.wait()
    high.wait()
    half.wait()


def target_kernel(
    pos_ref, own_ref, got_ref, gain_ref, far_w_ref, logits_ref, x_ref, w_ref, n_ref, sem
):
    weights = begin(far_w_ref, w_ref, sem.at[4])
    here = pos_ref[0]
    for source, which in ((got_ref, 0), (own_ref, 1)):

        @pl.when(here == which)
        def _(source=source):
            for i in range(4):
                part = pl.ds(i * 16, 16)
                begin(source.at[part], x_ref.at[part], sem.at[i])

    ready = []
    for i in range(4):
        part = pl.ds(i * 16, 16)
        ready.append([pltpu.make_async_copy(own_ref.at[part], x_ref.at[part], sem.at[i])])

    def put(p, value):
        n_ref[p] = value

    normalize_into(lambda p: x_ref[p], gain_ref, 64, TOK, put, ready)
    weights.wait()
    logits = row_dot(lambda p: n_ref[p], w_ref, TOK).T
    logits_ref[...] = logits


def early_kernel(
    pos_ref, far_w_ref, a_low_ref, a_high_ref, b_low_ref, b_high_ref, l_ref, w_ref, a_ref, b_ref, rows_ref, sem
):
    low, high = pl.ds(0, 32), pl.ds(32, 32)
    copies = [
        begin(far_w_ref, w_ref, sem.at[0]),
        begin(a_low_ref, a_ref.at[low], sem.at[1]),
        begin(a_high_ref, a_ref.at[high], sem.at[2]),
        begin(b_low_ref, b_ref.at[low], sem.at[3]),
        begin(b_high_ref, b_ref.at[high], sem.at[4]),
    ]
    g = pos_ref[0]
    acc = jnp.zeros((TOK, LANE), F32)
    for i in range(4):
        for n in ((0, 1, 3), (), (2, 4), ())[i]:
            copies[n].wait()
        group = range(i * 16, i * 16 + 16)
        lhs = jnp.concatenate(
            [jnp.concatenate([ref[p] for p in group], axis=1) for ref in (a_ref, b_ref)], axis=0
        )
        acc += dot(lhs, w_ref[i * 2048 : (i + 1) * 2048, :])
    rows_ref[pl.ds(pl.multiple_of(g * HALF, HALF), HALF), :] = acc[:HALF]
    rows_ref[pl.ds(pl.multiple_of((1 - g) * HALF, HALF), HALF), :] = acc[HALF:]
    l_ref[...] = rows_ref[...].T


def logits_kernel(
    pos_ref,
    shifts_ref,
    far_x_ref,
    gain_ref,
    far_w_ref,
    l0_ref,
    l1_ref,
    t_ref,
    far_n_ref,
    half_ref,
    l_ref,
    tk_ref,
    stat_ref,
    x_ref,
    w_ref,
    n_ref,
    sem,
):
    ready = []
    for i in range(4):
        part = pl.ds(i * 16, 16)
        pair = []
        for h in range(2):
            rows = pl.ds(h * HALF, HALF)
            pair.append(begin(far_x_ref.at[h, part], x_ref.at[part, rows], sem.at[7 + 2 * i + h]))
        ready.append(pair)
    weights = begin(far_w_ref, w_ref, sem.at[4])

    def put(p, value):
        n_ref[p] = value

    normalize_into(lambda p: x_ref[p], gain_ref, 64, TOK, put, ready)
    out = begin(n_ref, far_n_ref, sem.at[5])
    half = begin(n_ref.at[pl.ds((1 - pos_ref[1]) * 32, 32)], half_ref, sem.at[6])
    weights.wait()
    l_ref[...] = row_dot(lambda p: n_ref[p], w_ref, TOK).T
    stats = []
    for k, ref in enumerate((l0_ref, l1_ref, l_ref)):
        logits, wanted = ref[...], shift_lanes(t_ref[...], shifts_ref[k])
        tk_ref[k] = wanted
        peak = jnp.max(logits, axis=0, keepdims=True)
        top = jnp.max(wanted, axis=0, keepdims=True)
        logits, wanted = logits - peak, wanted - top
        target = jnp.exp(wanted)
        total = jnp.sum(jnp.exp(logits), axis=0, keepdims=True)
        mass = jnp.sum(target, axis=0, keepdims=True)
        cross = jnp.sum(target * (wanted - logits), axis=0, keepdims=True)
        stats += [peak, total, top, mass, cross]
    rows = jnp.concatenate(stats + [jnp.zeros((1, LANE), F32)], axis=0)
    for i in range(8):
        stat_ref[i] = rows
    out.wait()
    half.wait()


def combine(blocks):
    rows = []
    for k in range(STEPS):
        peaks, totals, tops, masses, crosses = [blocks[:, 5 * k + i, :] for i in range(5)]
        peak = jnp.max(peaks, axis=0, keepdims=True)
        top = jnp.max(tops, axis=0, keepdims=True)
        total = jnp.sum(totals * jnp.exp(peaks - peak), axis=0, keepdims=True)
        share = jnp.exp(tops - top)
        mass = jnp.sum(masses * share, axis=0, keepdims=True)
        moved = crosses + masses * ((tops - top) - (peaks - peak))
        cross = jnp.sum(moved * share, axis=0, keepdims=True)
        rows.append((peak, total, top, mass, cross))
    return rows


def middle_kernel(in_ref, out_ref):
    rows = []
    for item in combine(in_ref[...]):
        rows += list(item)
    rows = jnp.concatenate(rows + [jnp.zeros((1, LANE), F32)], axis=0)
    for i in range(16):
        out_ref[i] = rows


def grad_kernel(vocab_total, pos_ref, in_ref, mask_ref, l0_ref, l1_ref, l2_ref, tk_ref, grad_ref, kl_ref):
    g = pos_ref[0]
    mask = mask_ref[...]
    weight = mask * (vocab_total / (STEPS * BLK))
    scores = []
    for k, (peak, total, top, mass, cross) in enumerate(combine(in_ref[...])):
        soft = jnp.exp((l0_ref, l1_ref, l2_ref)[k][...] - peak) / total
        target = (jnp.exp(tk_ref[k] - top) / mass).astype(BF16).astype(F32)
        grad = weight * (soft - target)
        if k < 2:
            grad = pltpu.roll(grad, g * HALF, 1)
        grad_ref[k] = grad.astype(BF16)
        scores.append((cross / mass - jnp.log(mass) + jnp.log(total)) * mask)
    kl_ref[...] = jnp.concatenate(scores + [jnp.zeros((5, LANE), F32)], axis=0)


def head_kernel(pos_ref, g_ref, h_ref, *rest):
    far, (out_ref, x_ref, o_ref, sem) = rest[:16], rest[16:]
    core = pos_ref[1]
    groups = (far[0:2], far[2:4], far[4:6], far[6:8], far[8:9], far[9:10], far[10:12], far[12:13], far[13:15], far[15:16])

    def copies_of(q, which):
        at, copies = 0, []
        for n, refs in enumerate(groups):
            ref = refs[which] if len(refs) == 2 else refs[0]
            count = ref.shape[1]
            start = q * 8 + (which * 32 if ref.shape[0] == 64 else 0)
            target = x_ref.at[pl.ds(q * 8, 8), pl.ds(at, count)]
            copies.append(pltpu.make_async_copy(ref.at[pl.ds(start, 8)], target, sem.at[q, n]))
            at += count
        return copies

    for which in range(2):

        @pl.when(core == which)
        def _(which=which):
            for q in range(4):
                for copy in copies_of(q, which):
                    copy.start()

    copies = [copies_of(q, 0) for q in range(4)]
    lhs = jnp.concatenate(
        [g_ref[0], g_ref[1], g_ref[2], h_ref[0], h_ref[1], h_ref[2]], axis=1
    )
    outs = []
    for q in range(4):
        for copy in copies[q]:
            copy.wait()
        rhs = jnp.concatenate([x_ref[q * 8 + i] for i in range(8)], axis=1)
        grad = dot(lhs, rhs)
        for i in range(8):
            o_ref[q * 8 + i] = grad[:, i * LANE : (i + 1) * LANE].T.astype(BF16)
        part = pl.ds(q * 8, 8)
        outs.append(begin(o_ref.at[part], out_ref.at[part], sem.at[q, 10]))
    for copy in outs:
        copy.wait()


def on_device(
    feats,
    ids,
    loss_mask,
    owner,
    shifts,
    target_gain,
    target_head,
    fc_weight,
    embed,
    draft_gain,
    layer_weight,
    draft_head,
):
    g = lax.axis_index("xh")
    c = lax.axis_index("c")
    y, xl, z = lax.axis_index("y"), lax.axis_index("xl"), lax.axis_index("z")
    pos = jnp.stack([g, c, z]).astype(jnp.int32)
    vocab_total = LANE * 128
    target_gain = target_gain.reshape(4, 16, LANE)
    draft_gain = draft_gain.reshape(4, 16, LANE)

    level = jnp.where(g == 0, feats[:, 0, :], feats[:, 2, :])
    column = spread(level, "z").reshape(8 * TOK, LANE)

    mid = feats[:, 1, :]
    rounds = (
        ((0, 1), (1, 0), (6, 7), (7, 6)),
        ((0, 2), (1, 3), (6, 4), (7, 5)),
        ((0, 3), (1, 2), (6, 5), (7, 4)),
    )
    r1, r2, r3 = [lax.ppermute(mid, ("xh", "y"), list(pairs)) for pairs in rounds]
    holder, even = (y // 2) == g, (y % 2) == 0
    near, far = jnp.where(holder, mid, r2), jnp.where(holder, r1, r3)
    pair = jnp.stack([jnp.where(even, near, far), jnp.where(even, far, near)])
    pair_got = swap(pair, "xl")
    quad = jnp.stack([jnp.where(xl == 0, pair, pair_got), jnp.where(xl == 0, pair_got, pair)])
    seq_ids = lax.dynamic_slice_in_dim(ids, c * TOK, TOK, 0)
    local_ids = seq_ids - g * embed.shape[0]
    inside = (local_ids >= 0) & (local_ids < embed.shape[0])
    picked = jnp.take(embed, jnp.clip(local_ids, 0, embed.shape[0] - 1), axis=0)
    picked = jnp.where(inside[:, None], picked, jnp.zeros((), BF16)).reshape(2, HALF, LANE)
    e_own = lax.dynamic_index_in_dim(picked, g, 0, keepdims=False)
    e_got = swap(lax.dynamic_index_in_dim(picked, 1 - g, 0, keepdims=False), "xh")

    column, quad, e_got = lax.optimization_barrier((column, quad, e_got))
    wide = spread(column, ("y", "xl")).reshape(64, TOK, LANE)
    up = [(i, (i + 1) % 8) for i in range(8)]
    down = [(i, (i + 7) % 8) for i in range(8)]
    ring, a, b = [quad], quad, quad
    for _ in range(3):
        a, b = lax.ppermute(a, "z", up), lax.ppermute(b, "z", down)
        ring += [a, b]
    ring += [lax.ppermute(a[0:1], "z", up), lax.ppermute(b[1:2], "z", down)]

    own_part, other_part = call(
        unite_kernel,
        (sds((HALF, LANE), F32), sds((HALF, LANE), F32)),
        (SMEM,) + (ANY,) * 11,
        flops=2 * 128 * 12288 * 128,
        nbytes=6 << 20,
        scratch=[
            pltpu.VMEM((64, TOK, LANE), BF16),
            pltpu.VMEM((8192, LANE), BF16),
            pltpu.VMEM((8, 2, 2, TOK, LANE), BF16),
            pltpu.VMEM((4096, LANE), BF16),
            pltpu.VMEM((TOK, LANE), F32),
        ],
        sems=18,
    )(pos, wide, *ring, fc_weight)
    part_got = swap(other_part, "xh")

    high, part_got = lax.optimization_barrier((wide, part_got))
    high_got = across_grp(high, ((3, 0), (2, 1)))

    state, e_rows, mix = call(
        first_kernel,
        (sds((HALF, LANE), F32), sds((HALF, LANE), BF16), sds((64, HALF, LANE), BF16)),
        (SMEM, VMEM, VMEM, VMEM, VMEM),
        big=False,
    )(shifts, own_part, part_got, e_own, e_got)

    rows64 = pltpu.VMEM((64, HALF, LANE), BF16)
    rows128 = pltpu.VMEM((64, TOK, LANE), BF16)
    weights = pltpu.VMEM((8192, LANE), BF16)
    tp = ("y", "xl", "z")
    mine, theirs, halves = [], [], []
    for step in range(2):
        rows = lax.all_to_all(mix, tp, 0, 0, tiled=True)
        if step == 1:
            t_logits = call(
                target_kernel,
                (sds((LANE, TOK), F32),),
                (SMEM, ANY, ANY, VMEM, ANY),
                flops=2 * 128 * 8192 * 128,
                nbytes=4 << 20,
                scratch=[rows128, weights, rows128],
                sems=5,
            )(pos, wide, high_got, target_gain, target_head)[0]
            rows, t_logits = lax.optimization_barrier((rows, t_logits))
        low, high, half, state, mix = call(
            functools.partial(layer_kernel, step),
            (
                sds((32, HALF, LANE), BF16),
                sds((32, HALF, LANE), BF16),
                sds((32, HALF, LANE), BF16),
                sds((HALF, LANE), F32),
                sds((64 if step == 0 else 8, HALF, LANE), BF16),
            ),
            (SMEM, SMEM, ANY, VMEM, ANY, VMEM, VMEM),
            flops=2 * 64 * 8192 * 128,
            nbytes=4 << 20,
            scratch=[rows64, weights, rows64],
            sems=8,
            far=(0, 1, 2),
        )(pos, shifts, rows, draft_gain, layer_weight, state, e_rows)
        mine.append((low, high))
        halves.append(half)
        theirs.append((across_grp(low), across_grp(high)))

    part = lax.all_to_all(mix, "z", 0, 0, tiled=True).reshape(8 * HALF, LANE)
    part, theirs[0], first_part = lax.optimization_barrier((part, theirs[0], theirs[1][0]))
    theirs[1] = (first_part, theirs[1][1])
    last = spread(part, ("xh", "y", "xl")).reshape(2, 64, HALF, LANE)

    early = [
        call(
            early_kernel,
            (sds((LANE, TOK), F32),),
            (SMEM,) + (ANY,) * 5,
            flops=2 * 128 * 8192 * 128,
            nbytes=4 << 20,
            scratch=[weights, rows64, rows64, pltpu.VMEM((TOK, LANE), F32)],
            sems=5,
        )(pos, draft_head, *mine[k], *theirs[k])[0]
        for k in range(2)
    ]
    n_last, half, l_last, targets, stat = call(
        logits_kernel,
        (
            sds((64, TOK, LANE), BF16),
            sds((32, TOK, LANE), BF16),
            sds((LANE, TOK), F32),
            sds((STEPS, LANE, TOK), F32),
            sds((8, 16, LANE), F32),
        ),
        (SMEM, SMEM, ANY, VMEM, ANY, VMEM, VMEM, VMEM),
        flops=2 * 128 * 8192 * 128,
        nbytes=6 << 20,
        scratch=[rows128, weights, rows128],
        sems=15,
        far=(0, 1),
    )(pos, shifts, last, draft_gain, draft_head, early[0], early[1], t_logits)

    across = [swap(v, "c") for v in (halves[0], *theirs[0], halves[1], *theirs[1], half)]

    stat = lax.all_to_all(stat, "z", 0, 0, tiled=True)
    stat = call(middle_kernel, (sds((16, 16, LANE), F32),), (VMEM,), big=False)(stat)[0]
    stat = lax.all_to_all(stat, ("xh", "y", "xl"), 0, 0, tiled=True)

    mask = lax.dynamic_slice_in_dim(loss_mask, c * TOK, TOK, 0).astype(F32)[None, :]
    grads, kl = call(
        functools.partial(grad_kernel, vocab_total),
        (sds((STEPS, LANE, TOK), BF16), sds((8, LANE), F32)),
        (SMEM,) + (VMEM,) * 6,
        big=False,
    )(pos, stat, mask, early[0], early[1], l_last, targets)
    grads_got, kl_got = swap(grads, "c"), swap(kl, "c")

    head_grad = call(
        head_kernel,
        (sds((32, LANE, LANE), BF16),),
        (SMEM, VMEM, VMEM) + (ANY,) * 16,
        flops=2 * 768 * 4096 * 128,
        nbytes=8 << 20,
        scratch=[pltpu.VMEM((32, 768, LANE), BF16), pltpu.VMEM((32, LANE, LANE), BF16)]
        + [pltpu.SemaphoreType.DMA((4, 11))],
        far=(0,),
    )(
        pos,
        grads,
        grads_got,
        *mine[0],
        *theirs[0],
        *mine[1],
        *theirs[1],
        n_last,
        *across,
    )[0].reshape(4096, LANE)

    blocks = TOK // BLK
    kl_own, kl_other = kl[:STEPS], kl_got[:STEPS]
    kl_all = jnp.where(c == 0, jnp.stack([kl_own, kl_other], 1), jnp.stack([kl_other, kl_own], 1))
    kl_all = kl_all.reshape(STEPS, 2, 1, blocks, BLK)
    hits = (owner[:, 0].reshape(2, blocks) == c).astype(jnp.int32)
    rank = jnp.cumsum(hits, axis=1) - 1
    pick = (hits[:, None, :] > 0) & (
        rank[:, None, :] == jnp.arange(MOST, dtype=jnp.int32)[None, :, None]
    )
    slot_kl = jnp.sum(jnp.where(pick[None, :, :, :, None], kl_all, 0.0), axis=3)
    return head_grad, slot_kl.reshape(STEPS, 2 * MOST * BLK)


def solution(mesh):
    fine = Mesh(np.asarray(mesh.devices).reshape(2, 4, 2, 8, 2), ("xh", "y", "xl", "z", "c"))
    tp = ("y", "xl", "z")
    every = ("xh",) + tp
    return jax.shard_map(
        on_device,
        mesh=fine,
        in_specs=(
            P("c", None, tp),
            P(),
            P(),
            P(),
            P(),
            P(),
            P(None, every),
            P("xh", tp),
            P("xh", tp),
            P(),
            P(None, tp),
            P(None, every),
        ),
        out_specs=(P("c", every), P(None, "c")),
        check_vma=False,
    )
```

time: 342 us -> 256 us (0.75)
  blocking collectives: 77.5 us -> 0 us
  waiting for transfers between devices: 146 us -> 88.5 us
  starting transfers between devices: 54.7 us -> 106 us
  local copies, waits for them, and re-layouts: 30.7 us -> 13.1 us
  Pallas kernels: 26 us -> 41.7 us
    all_to_all x5 -> x0, blocking collectives: 77.5 us -> none  [the longest x3 49.5 us: spread(): lax.all_to_all(jnp.broadcast_to(values[None], (count,) + values.shape), a...]
    all_to_all x3, waiting for transfers between devices: 70.7 us -> 4.13 us  [spread(): lax.all_to_all(jnp.broadcast_to(values[None], (count,) + values.shape), a...]
    ppermute x12, waiting for transfers between devices: 67.2 us -> 8.67 us  [swap(): lax.ppermute(values, axis, [(i, (i + count // 2) % count) for i in range(...]
    ppermute x1 -> x16, waiting for transfers between devices: 0.01 us -> 47.3 us  [the longest x5 37.4 us: across_grp(): return lax.ppermute(values, ('xh', 'xl'), list(pairs))]
    all_to_all x0 -> x3, waiting for transfers between devices: none -> 26.5 us  [the longest x2 21.1 us: on_device(): rows = lax.all_to_all(mix, tp, 0, 0, tiled=True)]
    ppermute x1 -> x16, starting transfers between devices: 1.28 us -> 27.3 us  [the longest x3 9.23 us: on_device(): lax.ppermute(mid, ('xh', 'y'), list(pairs))]
    all_to_all x0 -> x3, starting transfers between devices: none -> 23 us  [the longest x2 17.5 us: on_device(): rows = lax.all_to_all(mix, tp, 0, 0, tiled=True)]
    pallas_call x6 -> x8, Pallas kernels: 20.6 us -> 34.5 us  [the longest x2 8.77 us: on_device(): call(functools.partial(layer_kernel, step), (sds((32, HALF, LANE), BF16),...]
  transfers between devices with their start and end apart: 18 -> 36, of which waited for: 10 -> 21; matrix products, arithmetic and copies ran while one was open for 5% -> 2% of each run, Pallas kernels for 3% -> 10%
where the time goes in v2:
time: 256 us; the launch traced here: 254 us
  starting transfers between devices  106 us (41%)
  waiting for transfers between devices  88.5 us (35%)
  Pallas kernels  41.7 us (16%)
  local copies, waits for them, and re-layouts  13.1 us (5%)
  other arithmetic  3.64 us (1%)
    ppermute x5, waiting for transfers between devices, across_grp(): return lax.ppermute(values, ('xh', 'xl'), list(pairs))  37.4 us
    ppermute x12, starting transfers between devices, swap(): lax.ppermute(values, axis, [(i, (i + count // 2) % count) for i in range(...  23.6 us
    all_to_all x2, waiting for transfers between devices, on_device(): rows = lax.all_to_all(mix, tp, 0, 0, tiled=True)  21.1 us
    all_to_all x2, starting transfers between devices, on_device(): rows = lax.all_to_all(mix, tp, 0, 0, tiled=True)  17.5 us
    all_to_all x3, starting transfers between devices, spread(): lax.all_to_all(jnp.broadcast_to(values[None], (count,) + values.shape), a...  17.1 us
    all_to_all x1, starting transfers between devices, on_device(): stat = lax.all_to_all(stat, 'z', 0, 0, tiled=True)  9.91 us
    ppermute x3, starting transfers between devices, on_device(): lax.ppermute(mid, ('xh', 'y'), list(pairs))  9.23 us
    pallas_call x2, Pallas kernels, on_device(): call(functools.partial(layer_kernel, step), (sds((32, HALF, LANE), BF16),...  8.77 us
  transfers between devices with their start and end apart: 36, of which 21 were waited for; matrix products, arithmetic and copies ran while one was open for 2% of the time, Pallas kernels for 10%

profile of v2, /device:TPU:1, one launch (start us, length us, event | category | flops | bytes accessed | tf_op | source)
XLA Modules:
  0.0 254.2 jit_solution(2342293943867794600)
XLA Ops:
  1.6 5.6 %collective-permute-start = (bf16[128,128]{1,0:T(8,128)(2,1)S(1)}, bf16[128,128]{1,0:T(8,128)(2,1)S(1)}, u32[]{:S(2)}, u32[]{:S(2)}) collective-permute-start(bf16[128,128]{1,0:T(8,128)(2,1)S(1)} %get-tuple-element.72), channel_id=1, source_target_pairs={{0,64},{32,96},{192,128},{224,160},{1,65},{33,97},{193,129},{225,1... | collective-permute-start | bytes 98312 | tf_op jit(solution)/shard_map/ppermute | solution.py:419
  11.6 8.2 %all-to-all-start = ((bf16[8,128,128]{2,1,0:T(8,128)(2,1)}), bf16[8,128,128]{2,1,0:T(8,128)(2,1)S(1)}, u32[]{:S(2)}, u32[]{:S(2)}) async-start(bf16[8,128,128]{2,1,0:T(8,128)(2,1)} %broadcast_in_dim.74), calls=%async_computation | async-start | bytes 524288 | tf_op jit(solution)/shard_map/all_to_all | solution.py:55
  31.6 4.4 %all-to-all-start.1 = ((bf16[8,1024,128]{2,1,0:T(8,128)(2,1)}), bf16[8,1024,128]{2,1,0:T(8,128)(2,1)}, u32[]{:S(2)}, u32[]{:S(2)}) async-start(bf16[8,1024,128]{2,1,0:T(8,128)(2,1)} %broadcast_in_dim.82), calls=%async_computation.1 | async-start | bytes 4194304 | tf_op jit(solution)/shard_map/all_to_all | solution.py:55
  60.0 4.6 %shard_map.131 = (f32[64,128]{1,0:T(8,128)}, f32[64,128]{1,0:T(8,128)}) custom-call(s32[3]{0:T(128)} %pad_add_fusion.pos_ref, bf16[64,128,128]{2,1,0:T(8,128)(2,1)} %bitcast.12.a_ref.own_ref, bf16[2,2,128,128]{3,2,1,0:T(8,128)(2,1)} %copy-done.18, bf16[2,2,128,128]{3,2,1,0:T(8,128)(2,1)} %copy-done.21, bf16[2,2,128,128]{3,2,1,0:T(8,128)(2,1)} %copy-done.22, ...), custom_call_target="tpu_custom_call" | custom-call | flops 402653184 | bytes 6291456 | tf_op jit(solution)/shard_map/pallas_call | solution.py:443
  72.9 9.0 %all-to-all-start.2 = ((bf16[64,64,128]{2,1,0:T(8,128)(2,1)}), bf16[64,64,128]{2,1,0:T(8,128)(2,1)S(1)}, u32[]{:S(2)}, u32[]{:S(2)}) async-start(bf16[64,64,128]{2,1,0:T(8,128)(2,1)} %get-tuple-element.40), calls=%async_computation.2 | async-start | bytes 2097152 | tf_op jit(solution)/shard_map/all_to_all | solution.py:476
  83.3 17.4 %all-to-all-done.2.far_x_ref = bf16[64,64,128]{2,1,0:T(8,128)(2,1)S(1)} async-done(((bf16[64,64,128]{2,1,0:T(8,128)(2,1)}), bf16[64,64,128]{2,1,0:T(8,128)(2,1)S(1)}, u32[]{:S(2)}, u32[]{:S(2)}) %all-to-all-start.2) | async-done | bytes 1048608 | tf_op jit(solution)/shard_map/all_to_all | solution.py:476
  101.7 4.5 %shard_map.133 = (bf16[32,64,128]{2,1,0:T(8,128)(2,1)}, bf16[32,64,128]{2,1,0:T(8,128)(2,1)}, bf16[32,64,128]{2,1,0:T(8,128)(2,1)}, f32[64,128]{1,0:T(8,128)}, bf16[64,64,128]{2,1,0:T(8,128)(2,1)}) custom-call(s32[3]{0:T(128)} %pad_add_fusion.pos_ref, s32[3]{0:T(128)} %shifts_ref.7, bf16[64,64,128]{2,1,0:T(8,128)(2,1)} %copy-done.12, ...), custom_call_target="tpu_custom_call" | custom-call | flops 134217728 | bytes 4194304 | tf_op jit(solution)/shard_map/pallas_call | solution.py:488
  106.2 8.6 %all-to-all-start.3 = ((bf16[64,64,128]{2,1,0:T(8,128)(2,1)}), bf16[64,64,128]{2,1,0:T(8,128)(2,1)S(1)}, u32[]{:S(2)}, u32[]{:S(2)}) async-start(bf16[64,64,128]{2,1,0:T(8,128)(2,1)} %get-tuple-element.43), calls=%async_computation.3 | async-start | bytes 2097152 | tf_op jit(solution)/shard_map/all_to_all | solution.py:476
  117.6 6.6 %collective-permute-done.14.got_ref = bf16[64,128,128]{2,1,0:T(8,128)(2,1)} collective-permute-done((bf16[64,128,128]{2,1,0:T(8,128)(2,1)}, bf16[64,128,128]{2,1,0:T(8,128)(2,1)}, u32[]{:S(2)}, u32[]{:S(2)}) %collective-permute-start.14) | collective-permute-done | bytes 2097184 | tf_op jit(solution)/shard_map/ppermute | solution.py:61
  124.2 5.4 %shard_map.134.t_ref = f32[128,128]{1,0:T(8,128)} custom-call(s32[3]{0:T(128)} %pad_add_fusion.pos_ref, bf16[64,128,128]{2,1,0:T(8,128)(2,1)} %bitcast.12.a_ref.own_ref, bf16[64,128,128]{2,1,0:T(8,128)(2,1)} %collective-permute-done.14.got_ref, bf16[4,16,128]{2,1,0:T(8,128)(2,1)} %bitcast.40, bf16[8192,128]{1,0:T(8,128)(2,1)} %far_w_ref.7), custom_call_target="tpu_custom_call" | custom-call | flops 268435456 | bytes 4194304 | tf_op jit(solution)/shard_map/pallas_call | solution.py:478
  138.8 5.4 %all-to-all-start.4 = ((bf16[8,64,128]{2,1,0:T(8,128)(2,1)}), bf16[8,64,128]{2,1,0:T(8,128)(2,1)S(1)}, u32[]{:S(2)}, u32[]{:S(2)}) async-start(bf16[8,64,128]{2,1,0:T(8,128)(2,1)} %get-tuple-element.47), calls=%async_computation.4 | async-start | bytes 262144 | tf_op jit(solution)/shard_map/all_to_all | solution.py:508
  146.7 5.5 %all-to-all-done.4 = bf16[8,64,128]{2,1,0:T(8,128)(2,1)S(1)} async-done(((bf16[8,64,128]{2,1,0:T(8,128)(2,1)}), bf16[8,64,128]{2,1,0:T(8,128)(2,1)S(1)}, u32[]{:S(2)}, u32[]{:S(2)}) %all-to-all-start.4) | async-done | bytes 131104 | tf_op jit(solution)/shard_map/all_to_all | solution.py:508
  152.1 5.8 %collective-permute-done.17.b_low_ref.rest_6_ = bf16[32,64,128]{2,1,0:T(8,128)(2,1)S(1)} collective-permute-done((bf16[32,64,128]{2,1,0:T(8,128)(2,1)}, bf16[32,64,128]{2,1,0:T(8,128)(2,1)S(1)}, u32[]{:S(2)}, u32[]{:S(2)}) %collective-permute-start.17) | collective-permute-done | bytes 524320 | tf_op jit(solution)/shard_map/ppermute | solution.py:61
  159.6 4.6 %all-to-all-start.5 = ((bf16[16,512,128]{2,1,0:T(8,128)(2,1)}), bf16[16,512,128]{2,1,0:T(8,128)(2,1)}, u32[]{:S(2)}, u32[]{:S(2)}) async-start(bf16[16,512,128]{2,1,0:T(8,128)(2,1)} %broadcast_in_dim.83), calls=%async_computation.5 | async-start | bytes 4194304 | tf_op jit(solution)/shard_map/all_to_all | solution.py:55
  166.7 4.3 %shard_map.136.l0_ref = f32[128,128]{1,0:T(8,128)} custom-call(s32[3]{0:T(128)} %pad_add_fusion.pos_ref, bf16[8192,128]{1,0:T(8,128)(2,1)} %far_w_ref.11, bf16[32,64,128]{2,1,0:T(8,128)(2,1)} %get-tuple-element.48.a_low_ref.rest_0_, bf16[32,64,128]{2,1,0:T(8,128)(2,1)} %get-tuple-element.49.a_high_ref.rest_1_, ...), custom_call_target="tpu_custom_call" | custom-call | flops 268435456 | bytes 4194304 | tf_op jit(solution)/shard_map/pallas_call | solution.py:514
  171.0 22.5 %collective-permute-done.18.b_high_ref.rest_7_ = bf16[32,64,128]{2,1,0:T(8,128)(2,1)S(1)} collective-permute-done((bf16[32,64,128]{2,1,0:T(8,128)(2,1)S(1)}, bf16[32,64,128]{2,1,0:T(8,128)(2,1)S(1)}, u32[]{:S(2)}, u32[]{:S(2)}) %collective-permute-start.18) | collective-permute-done | bytes 524320 | tf_op jit(solution)/shard_map/ppermute | solution.py:61
  194.3 4.3 %shard_map.137.l1_ref = f32[128,128]{1,0:T(8,128)} custom-call(s32[3]{0:T(128)} %pad_add_fusion.pos_ref, bf16[8192,128]{1,0:T(8,128)(2,1)} %far_w_ref.11, bf16[32,64,128]{2,1,0:T(8,128)(2,1)} %get-tuple-element.50.a_low_ref.rest_4_, bf16[32,64,128]{2,1,0:T(8,128)(2,1)} %get-tuple-element.54.a_high_ref.rest_5_, bf16[32,64,128]{2,1,0:T(8,128)(2,1)} %copy-done.14, ...), custom_call_target="tpu_custom_call" | custom-call | flops 268435456 | bytes 4194304 | tf_op jit(solution)/shard_map/pallas_call | solution.py:514
  198.7 5.6 %shard_map.138 = (bf16[64,128,128]{2,1,0:T(8,128)(2,1)}, bf16[32,128,128]{2,1,0:T(8,128)(2,1)}, f32[128,128]{1,0:T(8,128)}, f32[3,128,128]{2,1,0:T(8,128)}, f32[8,16,128]{2,1,0:T(8,128)}) custom-call(s32[3]{0:T(128)} %pad_add_fusion.pos_ref, s32[3]{0:T(128)} %shifts_ref.7, bf16[2,64,64,128]{3,2,1,0:T(8,128)(2,1)} %bitcast.17.far_x_ref, ...), custom_call_target="tpu_custom_call" | custom-call | flops 268435456 | bytes 6291456 | tf_op jit(solution)/shard_map/pallas_call | solution.py:525
  204.3 9.9 %all-to-all-start.6 = ((f32[8,16,128]{2,1,0:T(8,128)}), f32[8,16,128]{2,1,0:T(8,128)S(1)}, u32[]{:S(2)}, u32[]{:S(2)}) async-start(f32[8,16,128]{2,1,0:T(8,128)} %get-tuple-element.57), calls=%async_computation.6 | async-start | bytes 131072 | tf_op jit(solution)/shard_map/all_to_all | solution.py:544
  214.3 5.0 %collective-permute-start.20 = (bf16[32,64,128]{2,1,0:T(8,128)(2,1)}, bf16[32,64,128]{2,1,0:T(8,128)(2,1)}, u32[]{:S(2)}, u32[]{:S(2)}) collective-permute-start(bf16[32,64,128]{2,1,0:T(8,128)(2,1)} %get-tuple-element.62), channel_id=1, source_target_pairs={{0,1},{1,0},{2,3},{3,2},{4,5},{5,4},{6,7},{7,6},{8,9},{9,8},{10,11... | collective-permute-start | bytes 1572872 | tf_op jit(solution)/shard_map/ppermute | solution.py:66
  222.2 5.1 %all-to-all-start.7 = ((f32[16,16,128]{2,1,0:T(8,128)}), f32[16,16,128]{2,1,0:T(8,128)S(1)}, u32[]{:S(2)}, u32[]{:S(2)}) async-start(f32[16,16,128]{2,1,0:T(8,128)} %shard_map.139), calls=%async_computation.7 | async-start | bytes 262144 | tf_op jit(solution)/shard_map/all_to_all | solution.py:546
  227.7 6.3 %collective-permute-start.21 = (bf16[32,64,128]{2,1,0:T(8,128)(2,1)}, bf16[32,64,128]{2,1,0:T(8,128)(2,1)}, u32[]{:S(2)}, u32[]{:S(2)}) collective-permute-start(bf16[32,64,128]{2,1,0:T(8,128)(2,1)} %collective-permute-done.15.b_low_ref.rest_2_), channel_id=1, source_target_pairs={{0,1},{1,0},{2,3},{3,2},{4,5},{5,4},{6,7},{7,6},{8,9},{9,8},{10,11... | collective-permute-start | bytes 1572872 | tf_op jit(solution)/shard_map/ppermute | solution.py:66
  236.7 7.5 %collective-permute-start.27 = (f32[8,128]{1,0:T(8,128)S(1)}, f32[8,128]{1,0:T(8,128)S(1)}, u32[]{:S(2)}, u32[]{:S(2)}) collective-permute-start(f32[8,128]{1,0:T(8,128)S(1)} %get-tuple-element.65), channel_id=1, source_target_pairs={{0,1},{1,0},{2,3},{3,2},{4,5},{5,4},{6,7},{7,6},{8,9},{9,8},{10,11... | collective-permute-start | bytes 12296 | tf_op jit(solution)/shard_map/ppermute | solution.py:66
  248.6 5.5 %shard_map.141 = bf16[32,128,128]{2,1,0:T(8,128)(2,1)} custom-call(s32[3]{0:T(128)} %pad_add_fusion.pos_ref, bf16[3,128,128]{2,1,0:T(8,128)(2,1)} %copy-done.4, bf16[3,128,128]{2,1,0:T(8,128)(2,1)} %copy-done.25, bf16[32,64,128]{2,1,0:T(8,128)(2,1)} %get-tuple-element.48.a_low_ref.rest_0_, bf16[32,64,128]{2,1,0:T(8,128)(2,1)} %get-tuple-element.49.a_high_ref.rest_1_, ...), custom_call_target="tpu_custom_call" | custom-call | flops 805306368 | bytes 8388608 | tf_op jit(solution)/shard_map/pallas_call | solution.py:557
  (150 shorter events, 81.4 us)
Async XLA Ops:
  1.6 20.0 %collective-permute-start = (bf16[128,128]{1,0:T(8,128)(2,1)S(1)}, bf16[128,128]{1,0:T(8,128)(2,1)S(1)}, u32[]{:S(2)}, u32[]{:S(2)}) collective-permute-start(bf16[128,128]{1,0:T(8,128)(2,1)S(1)} %get-tuple-element.72), channel_id=1, source_target_pairs={{0,64},{32,96},{192,128},{224,160},{1,65},{33,97},{193,129},{225,1... | collective-permute-start | bytes 98312 | tf_op jit(solution)/shard_map/ppermute | solution.py:419
  7.2 14.3 %collective-permute-start.1 = (bf16[128,128]{1,0:T(8,128)(2,1)S(1)}, bf16[128,128]{1,0:T(8,128)(2,1)S(1)}, u32[]{:S(2)}, u32[]{:S(2)}) collective-permute-start(bf16[128,128]{1,0:T(8,128)(2,1)S(1)} %get-tuple-element.72), channel_id=1, source_target_pairs={{0,32},{32,0},{192,224},{224,192},{1,33},{33,1},{193,225},{225,193... | collective-permute-start | bytes 98312 | tf_op jit(solution)/shard_map/ppermute | solution.py:419
  9.6 12.0 %collective-permute-start.2 = (bf16[128,128]{1,0:T(8,128)(2,1)S(1)}, bf16[128,128]{1,0:T(8,128)(2,1)S(1)}, u32[]{:S(2)}, u32[]{:S(2)}) collective-permute-start(bf16[128,128]{1,0:T(8,128)(2,1)S(1)} %get-tuple-element.72), channel_id=1, source_target_pairs={{0,96},{32,64},{192,160},{224,128},{1,97},{33,65},{193,161},{225,1... | collective-permute-start | bytes 98312 | tf_op jit(solution)/shard_map/ppermute | solution.py:419
  11.6 18.3 %all-to-all-start = ((bf16[8,128,128]{2,1,0:T(8,128)(2,1)}), bf16[8,128,128]{2,1,0:T(8,128)(2,1)S(1)}, u32[]{:S(2)}, u32[]{:S(2)}) async-start(bf16[8,128,128]{2,1,0:T(8,128)(2,1)} %broadcast_in_dim.74), calls=%async_computation | async-start | bytes 524288 | tf_op jit(solution)/shard_map/all_to_all | solution.py:55
  31.6 28.4 %all-to-all-start.1 = ((bf16[8,1024,128]{2,1,0:T(8,128)(2,1)}), bf16[8,1024,128]{2,1,0:T(8,128)(2,1)}, u32[]{:S(2)}, u32[]{:S(2)}) async-start(bf16[8,1024,128]{2,1,0:T(8,128)(2,1)} %broadcast_in_dim.82), calls=%async_computation.1 | async-start | bytes 4194304 | tf_op jit(solution)/shard_map/all_to_all | solution.py:55
  46.5 5.7 %collective-permute-start.9 = (bf16[2,2,128,128]{3,2,1,0:T(8,128)(2,1)S(1)}, bf16[2,2,128,128]{3,2,1,0:T(8,128)(2,1)S(1)}, u32[]{:S(2)}, u32[]{:S(2)}) collective-permute-start(bf16[2,2,128,128]{3,2,1,0:T(8,128)(2,1)S(1)} %collective-permute-done.7.rest_3_), channel_id=1, source_target_pairs={{0,2},{2,4},{4,6},{6,8},{8,10},{10,12},{12,14},{14,0},{1,3},{3,5},... | collective-permute-start | bytes 393224 | tf_op jit(solution)/shard_map/ppermute | solution.py:439
  46.5 5.8 %collective-permute-start.10 = (bf16[2,2,128,128]{3,2,1,0:T(8,128)(2,1)S(1)}, bf16[2,2,128,128]{3,2,1,0:T(8,128)(2,1)S(1)}, u32[]{:S(2)}, u32[]{:S(2)}) collective-permute-start(bf16[2,2,128,128]{3,2,1,0:T(8,128)(2,1)S(1)} %collective-permute-done.8.rest_4_), channel_id=1, source_target_pairs={{0,14},{2,0},{4,2},{6,4},{8,6},{10,8},{12,10},{14,12},{1,15},{3,1}... | collective-permute-start | bytes 393224 | tf_op jit(solution)/shard_map/ppermute | solution.py:439
  52.2 5.4 %collective-permute-start.11 = (bf16[1,2,128,128]{3,2,1,0:T(8,128)(2,1)S(1)}, bf16[1,2,128,128]{3,2,1,0:T(8,128)(2,1)S(1)}, u32[]{:S(2)}, u32[]{:S(2)}) collective-permute-start(bf16[1,2,128,128]{3,2,1,0:T(8,128)(2,1)S(1)} %slice.30), channel_id=1, source_target_pairs={{0,2},{2,4},{4,6},{6,8},{8,10},{10,12},{12,14},{14,0},{1,3},{3,5},... | collective-permute-start | bytes 196616 | tf_op jit(solution)/shard_map/ppermute | solution.py:441
  72.9 27.8 %all-to-all-start.2 = ((bf16[64,64,128]{2,1,0:T(8,128)(2,1)}), bf16[64,64,128]{2,1,0:T(8,128)(2,1)S(1)}, u32[]{:S(2)}, u32[]{:S(2)}) async-start(bf16[64,64,128]{2,1,0:T(8,128)(2,1)} %get-tuple-element.40), calls=%async_computation.2 | async-start | bytes 2097152 | tf_op jit(solution)/shard_map/all_to_all | solution.py:476
  81.9 42.3 %collective-permute-start.14 = (bf16[64,128,128]{2,1,0:T(8,128)(2,1)}, bf16[64,128,128]{2,1,0:T(8,128)(2,1)}, u32[]{:S(2)}, u32[]{:S(2)}) collective-permute-start(bf16[64,128,128]{2,1,0:T(8,128)(2,1)} %bitcast.12.a_ref.own_ref), channel_id=1, source_target_pairs={{144,0},{128,16},{145,1},{129,17},{146,2},{130,18},{147,3},{131,19... | collective-permute-start | bytes 6291464 | tf_op jit(solution)/shard_map/ppermute | solution.py:61
  106.2 27.1 %all-to-all-start.3 = ((bf16[64,64,128]{2,1,0:T(8,128)(2,1)}), bf16[64,64,128]{2,1,0:T(8,128)(2,1)S(1)}, u32[]{:S(2)}, u32[]{:S(2)}) async-start(bf16[64,64,128]{2,1,0:T(8,128)(2,1)} %get-tuple-element.43), calls=%async_computation.3 | async-start | bytes 2097152 | tf_op jit(solution)/shard_map/all_to_all | solution.py:476
  114.8 29.4 %collective-permute-start.15 = (bf16[32,64,128]{2,1,0:T(8,128)(2,1)}, bf16[32,64,128]{2,1,0:T(8,128)(2,1)}, u32[]{:S(2)}, u32[]{:S(2)}) collective-permute-start(bf16[32,64,128]{2,1,0:T(8,128)(2,1)} %get-tuple-element.48.a_low_ref.rest_0_), channel_id=1, source_target_pairs={{0,144},{16,128},{128,16},{144,0},{1,145},{17,129},{129,17},{145,1... | collective-permute-start | bytes 1572872 | tf_op jit(solution)/shard_map/ppermute | solution.py:61
  115.3 31.4 %collective-permute-start.16 = (bf16[32,64,128]{2,1,0:T(8,128)(2,1)}, bf16[32,64,128]{2,1,0:T(8,128)(2,1)}, u32[]{:S(2)}, u32[]{:S(2)}) collective-permute-start(bf16[32,64,128]{2,1,0:T(8,128)(2,1)} %get-tuple-element.49.a_high_ref.rest_1_), channel_id=1, source_target_pairs={{0,144},{16,128},{128,16},{144,0},{1,145},{17,129},{129,17},{145,1... | collective-permute-start | bytes 1572872 | tf_op jit(solution)/shard_map/ppermute | solution.py:61
  138.5 19.4 %collective-permute-start.17 = (bf16[32,64,128]{2,1,0:T(8,128)(2,1)}, bf16[32,64,128]{2,1,0:T(8,128)(2,1)S(1)}, u32[]{:S(2)}, u32[]{:S(2)}) collective-permute-start(bf16[32,64,128]{2,1,0:T(8,128)(2,1)} %get-tuple-element.50.a_low_ref.rest_4_), channel_id=1, source_target_pairs={{0,144},{16,128},{128,16},{144,0},{1,145},{17,129},{129,17},{145,1... | collective-permute-start | bytes 1572872 | tf_op jit(solution)/shard_map/ppermute | solution.py:61
  138.8 13.4 %all-to-all-start.4 = ((bf16[8,64,128]{2,1,0:T(8,128)(2,1)}), bf16[8,64,128]{2,1,0:T(8,128)(2,1)S(1)}, u32[]{:S(2)}, u32[]{:S(2)}) async-start(bf16[8,64,128]{2,1,0:T(8,128)(2,1)} %get-tuple-element.47), calls=%async_computation.4 | async-start | bytes 262144 | tf_op jit(solution)/shard_map/all_to_all | solution.py:508
  159.6 39.0 %all-to-all-start.5 = ((bf16[16,512,128]{2,1,0:T(8,128)(2,1)}), bf16[16,512,128]{2,1,0:T(8,128)(2,1)}, u32[]{:S(2)}, u32[]{:S(2)}) async-start(bf16[16,512,128]{2,1,0:T(8,128)(2,1)} %broadcast_in_dim.83), calls=%async_computation.5 | async-start | bytes 4194304 | tf_op jit(solution)/shard_map/all_to_all | solution.py:55
  164.2 29.3 %collective-permute-start.18 = (bf16[32,64,128]{2,1,0:T(8,128)(2,1)S(1)}, bf16[32,64,128]{2,1,0:T(8,128)(2,1)S(1)}, u32[]{:S(2)}, u32[]{:S(2)}) collective-permute-start(bf16[32,64,128]{2,1,0:T(8,128)(2,1)S(1)} %copy-done.13), channel_id=1, source_target_pairs={{0,144},{16,128},{128,16},{144,0},{1,145},{17,129},{129,17},{145,1... | collective-permute-start | bytes 1572872 | tf_op jit(solution)/shard_map/ppermute | solution.py:61
  204.3 17.1 %all-to-all-start.6 = ((f32[8,16,128]{2,1,0:T(8,128)}), f32[8,16,128]{2,1,0:T(8,128)S(1)}, u32[]{:S(2)}, u32[]{:S(2)}) async-start(f32[8,16,128]{2,1,0:T(8,128)} %get-tuple-element.57), calls=%async_computation.6 | async-start | bytes 131072 | tf_op jit(solution)/shard_map/all_to_all | solution.py:544
  214.3 30.0 %collective-permute-start.20 = (bf16[32,64,128]{2,1,0:T(8,128)(2,1)}, bf16[32,64,128]{2,1,0:T(8,128)(2,1)}, u32[]{:S(2)}, u32[]{:S(2)}) collective-permute-start(bf16[32,64,128]{2,1,0:T(8,128)(2,1)} %get-tuple-element.62), channel_id=1, source_target_pairs={{0,1},{1,0},{2,3},{3,2},{4,5},{5,4},{6,7},{7,6},{8,9},{9,8},{10,11... | collective-permute-start | bytes 1572872 | tf_op jit(solution)/shard_map/ppermute | solution.py:66
  219.3 25.1 %collective-permute-start.23 = (bf16[32,64,128]{2,1,0:T(8,128)(2,1)}, bf16[32,64,128]{2,1,0:T(8,128)(2,1)}, u32[]{:S(2)}, u32[]{:S(2)}) collective-permute-start(bf16[32,64,128]{2,1,0:T(8,128)(2,1)} %get-tuple-element.63), channel_id=1, source_target_pairs={{0,1},{1,0},{2,3},{3,2},{4,5},{5,4},{6,7},{7,6},{8,9},{9,8},{10,11... | collective-permute-start | bytes 1572872 | tf_op jit(solution)/shard_map/ppermute | solution.py:66
  219.6 28.3 %collective-permute-start.26 = (bf16[32,128,128]{2,1,0:T(8,128)(2,1)}, bf16[32,128,128]{2,1,0:T(8,128)(2,1)}, u32[]{:S(2)}, u32[]{:S(2)}) collective-permute-start(bf16[32,128,128]{2,1,0:T(8,128)(2,1)} %get-tuple-element.64), channel_id=1, source_target_pairs={{0,1},{1,0},{2,3},{3,2},{4,5},{5,4},{6,7},{7,6},{8,9},{9,8},{10,11... | collective-permute-start | bytes 3145736 | tf_op jit(solution)/shard_map/ppermute | solution.py:66
  222.2 11.9 %all-to-all-start.7 = ((f32[16,16,128]{2,1,0:T(8,128)}), f32[16,16,128]{2,1,0:T(8,128)S(1)}, u32[]{:S(2)}, u32[]{:S(2)}) async-start(f32[16,16,128]{2,1,0:T(8,128)} %shard_map.139), calls=%async_computation.7 | async-start | bytes 262144 | tf_op jit(solution)/shard_map/all_to_all | solution.py:546
  227.7 17.9 %collective-permute-start.21 = (bf16[32,64,128]{2,1,0:T(8,128)(2,1)}, bf16[32,64,128]{2,1,0:T(8,128)(2,1)}, u32[]{:S(2)}, u32[]{:S(2)}) collective-permute-start(bf16[32,64,128]{2,1,0:T(8,128)(2,1)} %collective-permute-done.15.b_low_ref.rest_2_), channel_id=1, source_target_pairs={{0,1},{1,0},{2,3},{3,2},{4,5},{5,4},{6,7},{7,6},{8,9},{9,8},{10,11... | collective-permute-start | bytes 1572872 | tf_op jit(solution)/shard_map/ppermute | solution.py:66
  236.7 8.3 %collective-permute-start.27 = (f32[8,128]{1,0:T(8,128)S(1)}, f32[8,128]{1,0:T(8,128)S(1)}, u32[]{:S(2)}, u32[]{:S(2)}) collective-permute-start(f32[8,128]{1,0:T(8,128)S(1)} %get-tuple-element.65), channel_id=1, source_target_pairs={{0,1},{1,0},{2,3},{3,2},{4,5},{5,4},{6,7},{7,6},{8,9},{9,8},{10,11... | collective-permute-start | bytes 12296 | tf_op jit(solution)/shard_map/ppermute | solution.py:66
  (42 other events, 453.8 us)

commit v3 on v2

--- a/solution.py
+++ b/solution.py
@@ -112,11 +112,13 @@
     other_ref[...] = acc_ref[pl.ds(pl.multiple_of((1 - g) * HALF, HALF), HALF), :]
 
 
-def first_kernel(shifts_ref, own_ref, got_ref, e_own_ref, e_got_ref, state_ref, e_ref, mix_ref):
+def first_state(own_ref, got_ref, e_own_ref, e_got_ref):
     state = (own_ref[...] + got_ref[...]).astype(BF16).astype(F32)
-    state_ref[...] = state
-    rows = (e_own_ref[...].astype(F32) + e_got_ref[...].astype(F32)).astype(BF16)
-    e_ref[...] = rows
+    return state, (e_own_ref[...].astype(F32) + e_got_ref[...].astype(F32)).astype(BF16)
+
+
+def first_kernel(shifts_ref, own_ref, got_ref, e_own_ref, e_got_ref, mix_ref):
+    state, rows = first_state(own_ref, got_ref, e_own_ref, e_got_ref)
     mixed = (state + dot(shift_rows(shifts_ref[0], HALF), rows)).astype(BF16)
     for i in range(64):
         mix_ref[i] = mixed
@@ -146,25 +148,11 @@
     return acc
 
 
-def layer_kernel(
-    step,
-    pos_ref,
-    shifts_ref,
-    far_x_ref,
-    gain_ref,
-    far_w_ref,
-    state_ref,
-    e_ref,
-    low_ref,
-    high_ref,
-    half_ref,
-    next_ref,
-    mix_ref,
-    x_ref,
-    w_ref,
-    n_ref,
-    sem,
-):
+def layer_kernel(step, shifts_ref, far_x_ref, gain_ref, far_w_ref, *rest):
+    if step == 0:
+        parts, (low_ref, high_ref, next_ref, e_ref, mix_ref, x_ref, w_ref, n_ref, sem) = rest[:4], rest[4:]
+    else:
+        state_ref, e_ref, low_ref, high_ref, mix_ref, x_ref, w_ref, n_ref, sem = rest
     ready = []
     for i in range(4):
         part = pl.ds(i * 16, 16)
@@ -176,14 +164,18 @@
 
     normalize_into(lambda p: x_ref[p], gain_ref, 64, HALF, put, ready)
     low = begin(n_ref.at[pl.ds(0, 32)], low_ref, sem.at[5])
-    high = begin(n_ref.at[pl.ds(32, 32)], high_ref, sem.at[7])
-    half = begin(n_ref.at[pl.ds((1 - pos_ref[1]) * 32, 32)], half_ref, sem.at[6])
+    high = begin(n_ref.at[pl.ds(32, 32)], high_ref, sem.at[6])
+    if step == 0:
+        state, rows = first_state(*parts)
+        e_ref[...] = rows
+    else:
+        state, rows = state_ref[...], e_ref[...]
     weights.wait()
     acc = row_dot(lambda p: n_ref[p], w_ref, HALF)
-    state = state_ref[...] + acc * jax.nn.sigmoid(acc)
-    next_ref[...] = state
-    mixed = (state + dot(shift_rows(shifts_ref[step + 1], HALF), e_ref[...])).astype(BF16)
+    state = state + acc * jax.nn.sigmoid(acc)
+    mixed = (state + dot(shift_rows(shifts_ref[step + 1], HALF), rows)).astype(BF16)
     if step == 0:
+        next_ref[...] = state
         for i in range(64):
             mix_ref[i] = mixed
     else:
@@ -191,7 +183,6 @@
             mix_ref[i] = mixed
     low.wait()
     high.wait()
-    half.wait()
 
 
 def target_kernel(
@@ -247,25 +238,11 @@
     l_ref[...] = rows_ref[...].T
 
 
-def logits_kernel(
-    pos_ref,
-    shifts_ref,
-    far_x_ref,
-    gain_ref,
-    far_w_ref,
-    l0_ref,
-    l1_ref,
-    t_ref,
-    far_n_ref,
-    half_ref,
-    l_ref,
-    tk_ref,
-    stat_ref,
-    x_ref,
-    w_ref,
-    n_ref,
-    sem,
-):
+def logits_kernel(pos_ref, shifts_ref, far_x_ref, gain_ref, far_w_ref, l0_ref, t_ref, *rest):
+    far, (low_ref, high_ref, l1_ref, l_ref, tk_ref, stat_ref, x_ref, w_ref, n_ref, r_ref, sem) = (
+        rest[:4],
+        rest[4:],
+    )
     ready = []
     for i in range(4):
         part = pl.ds(i * 16, 16)
@@ -275,15 +252,28 @@
             pair.append(begin(far_x_ref.at[h, part], x_ref.at[part, rows], sem.at[7 + 2 * i + h]))
         ready.append(pair)
     weights = begin(far_w_ref, w_ref, sem.at[4])
+    second = []
+    for n, ref in enumerate(far):
+        target = r_ref.at[pl.ds(n % 2 * 32, 32), pl.ds(n // 2 * HALF, HALF)]
+        second.append(begin(ref, target, sem.at[15 + n]))
 
     def put(p, value):
         n_ref[p] = value
 
     normalize_into(lambda p: x_ref[p], gain_ref, 64, TOK, put, ready)
-    out = begin(n_ref, far_n_ref, sem.at[5])
-    half = begin(n_ref.at[pl.ds((1 - pos_ref[1]) * 32, 32)], half_ref, sem.at[6])
-    weights.wait()
-    l_ref[...] = row_dot(lambda p: n_ref[p], w_ref, TOK).T
+    low = begin(n_ref.at[pl.ds(0, 32)], low_ref, sem.at[5])
+    high = begin(n_ref.at[pl.ds(32, 32)], high_ref, sem.at[6])
+    for copy in [weights] + second:
+        copy.wait()
+    acc = jnp.zeros((2 * TOK, LANE), F32)
+    for i in range(4):
+        group = range(i * 16, i * 16 + 16)
+        lhs = jnp.concatenate(
+            [jnp.concatenate([ref[p] for p in group], axis=1) for ref in (n_ref, r_ref)], axis=0
+        )
+        acc += dot(lhs, w_ref[i * 2048 : (i + 1) * 2048, :])
+    l_ref[...] = acc[:TOK].T
+    l1_ref[...] = pltpu.roll(acc[TOK:].T, pos_ref[0] * HALF, 1)
     stats = []
     for k, ref in enumerate((l0_ref, l1_ref, l_ref)):
         logits, wanted = ref[...], shift_lanes(t_ref[...], shifts_ref[k])
@@ -299,8 +289,8 @@
     rows = jnp.concatenate(stats + [jnp.zeros((1, LANE), F32)], axis=0)
     for i in range(8):
         stat_ref[i] = rows
-    out.wait()
-    half.wait()
+    low.wait()
+    high.wait()
 
 
 def combine(blocks):
@@ -327,13 +317,14 @@
         out_ref[i] = rows
 
 
-def grad_kernel(vocab_total, pos_ref, in_ref, mask_ref, l0_ref, l1_ref, l2_ref, tk_ref, grad_ref, kl_ref):
+def grad_kernel(vocab_total, pos_ref, in_ref, mask_ref, *rest):
+    l_refs, (tk_ref, grad_ref, kl_ref) = rest[:3], rest[3:]
     g = pos_ref[0]
     mask = mask_ref[...]
     weight = mask * (vocab_total / (STEPS * BLK))
     scores = []
     for k, (peak, total, top, mass, cross) in enumerate(combine(in_ref[...])):
-        soft = jnp.exp((l0_ref, l1_ref, l2_ref)[k][...] - peak) / total
+        soft = jnp.exp(l_refs[k][...] - peak) / total
         target = (jnp.exp(tk_ref[k] - top) / mass).astype(BF16).astype(F32)
         grad = weight * (soft - target)
         if k < 2:
@@ -344,16 +335,15 @@
 
 
 def head_kernel(pos_ref, g_ref, h_ref, *rest):
-    far, (out_ref, x_ref, o_ref, sem) = rest[:16], rest[16:]
+    far, (out_ref, x_ref, o_ref, sem) = rest[:20], rest[20:]
     core = pos_ref[1]
-    groups = (far[0:2], far[2:4], far[4:6], far[6:8], far[8:9], far[9:10], far[10:12], far[12:13], far[13:15], far[15:16])
 
     def copies_of(q, which):
         at, copies = 0, []
-        for n, refs in enumerate(groups):
-            ref = refs[which] if len(refs) == 2 else refs[0]
+        for n in range(10):
+            ref = far[2 * n + which]
             count = ref.shape[1]
-            start = q * 8 + (which * 32 if ref.shape[0] == 64 else 0)
+            start = q * 8
             target = x_ref.at[pl.ds(q * 8, 8), pl.ds(at, count)]
             copies.append(pltpu.make_async_copy(ref.at[pl.ds(start, 8)], target, sem.at[q, n]))
             at += count
@@ -460,90 +450,94 @@
     high, part_got = lax.optimization_barrier((wide, part_got))
     high_got = across_grp(high, ((3, 0), (2, 1)))
 
-    state, e_rows, mix = call(
+    mix = call(
         first_kernel,
-        (sds((HALF, LANE), F32), sds((HALF, LANE), BF16), sds((64, HALF, LANE), BF16)),
+        (sds((64, HALF, LANE), BF16),),
         (SMEM, VMEM, VMEM, VMEM, VMEM),
         big=False,
-    )(shifts, own_part, part_got, e_own, e_got)
+    )(shifts, own_part, part_got, e_own, e_got)[0]
 
     rows64 = pltpu.VMEM((64, HALF, LANE), BF16)
     rows128 = pltpu.VMEM((64, TOK, LANE), BF16)
     weights = pltpu.VMEM((8192, LANE), BF16)
     tp = ("y", "xl", "z")
-    mine, theirs, halves = [], [], []
+    mine, theirs = [], []
     for step in range(2):
         rows = lax.all_to_all(mix, tp, 0, 0, tiled=True)
         if step == 1:
-            t_logits = call(
-                target_kernel,
-                (sds((LANE, TOK), F32),),
-                (SMEM, ANY, ANY, VMEM, ANY),
-                flops=2 * 128 * 8192 * 128,
-                nbytes=4 << 20,
-                scratch=[rows128, weights, rows128],
-                sems=5,
-            )(pos, wide, high_got, target_gain, target_head)[0]
-            rows, t_logits = lax.optimization_barrier((rows, t_logits))
-        low, high, half, state, mix = call(
+            rows, high_got = lax.optimization_barrier((rows, high_got))
+        held = (own_part, part_got, e_own, e_got) if step == 0 else (state, e_rows)
+        rows32 = sds((32, HALF, LANE), BF16)
+        kept = (sds((HALF, LANE), F32), sds((HALF, LANE), BF16)) if step == 0 else ()
+        low, high, *kept, mix = call(
             functools.partial(layer_kernel, step),
-            (
-                sds((32, HALF, LANE), BF16),
-                sds((32, HALF, LANE), BF16),
-                sds((32, HALF, LANE), BF16),
-                sds((HALF, LANE), F32),
-                sds((64 if step == 0 else 8, HALF, LANE), BF16),
-            ),
-            (SMEM, SMEM, ANY, VMEM, ANY, VMEM, VMEM),
+            (rows32, rows32, *kept, sds((64 if step == 0 else 8, HALF, LANE), BF16)),
+            (SMEM, ANY, VMEM, ANY) + (VMEM,) * len(held),
             flops=2 * 64 * 8192 * 128,
             nbytes=4 << 20,
             scratch=[rows64, weights, rows64],
-            sems=8,
-            far=(0, 1, 2),
-        )(pos, shifts, rows, draft_gain, layer_weight, state, e_rows)
+            sems=7,
+            far=(0, 1),
+        )(shifts, rows, draft_gain, layer_weight, *held)
+        if step == 0:
+            state, e_rows = kept
         mine.append((low, high))
-        halves.append(half)
         theirs.append((across_grp(low), across_grp(high)))
 
     part = lax.all_to_all(mix, "z", 0, 0, tiled=True).reshape(8 * HALF, LANE)
-    part, theirs[0], first_part = lax.optimization_barrier((part, theirs[0], theirs[1][0]))
-    theirs[1] = (first_part, theirs[1][1])
+    t_logits = call(
+        target_kernel,
+        (sds((LANE, TOK), F32),),
+        (SMEM, ANY, ANY, VMEM, ANY),
+        flops=2 * 128 * 8192 * 128,
+        nbytes=4 << 20,
+        scratch=[rows128, weights, rows128],
+        sems=5,
+    )(pos, wide, high_got, target_gain, target_head)[0]
+    first_low, t_logits = lax.optimization_barrier((theirs[0][0], t_logits))
+    theirs[0] = (first_low, theirs[0][1])
+    l_first = call(
+        early_kernel,
+        (sds((LANE, TOK), F32),),
+        (SMEM,) + (ANY,) * 5,
+        flops=2 * 128 * 8192 * 128,
+        nbytes=4 << 20,
+        scratch=[weights, rows64, rows64, pltpu.VMEM((TOK, LANE), F32)],
+        sems=5,
+    )(pos, draft_head, *mine[0], *theirs[0])[0]
+    part, low, t_logits, l_first = lax.optimization_barrier(
+        (part, theirs[1][0], t_logits, l_first)
+    )
+    theirs[1] = (low, theirs[1][1])
     last = spread(part, ("xh", "y", "xl")).reshape(2, 64, HALF, LANE)
 
-    early = [
-        call(
-            early_kernel,
-            (sds((LANE, TOK), F32),),
-            (SMEM,) + (ANY,) * 5,
-            flops=2 * 128 * 8192 * 128,
-            nbytes=4 << 20,
-            scratch=[weights, rows64, rows64, pltpu.VMEM((TOK, LANE), F32)],
-            sems=5,
-        )(pos, draft_head, *mine[k], *theirs[k])[0]
-        for k in range(2)
-    ]
-    n_last, half, l_last, targets, stat = call(
+    n_low, n_high, l_second, l_last, targets, stat = call(
         logits_kernel,
         (
-            sds((64, TOK, LANE), BF16),
             sds((32, TOK, LANE), BF16),
+            sds((32, TOK, LANE), BF16),
+            sds((LANE, TOK), F32),
             sds((LANE, TOK), F32),
             sds((STEPS, LANE, TOK), F32),
             sds((8, 16, LANE), F32),
         ),
-        (SMEM, SMEM, ANY, VMEM, ANY, VMEM, VMEM, VMEM),
+        (SMEM, SMEM, ANY, VMEM, ANY, VMEM, VMEM) + (ANY,) * 4,
         flops=2 * 128 * 8192 * 128,
         nbytes=6 << 20,
-        scratch=[rows128, weights, rows128],
-        sems=15,
+        scratch=[rows128, weights, rows128, rows128],
+        sems=19,
         far=(0, 1),
-    )(pos, shifts, last, draft_gain, draft_head, early[0], early[1], t_logits)
-
-    across = [swap(v, "c") for v in (halves[0], *theirs[0], halves[1], *theirs[1], half)]
+    )(pos, shifts, last, draft_gain, draft_head, l_first, t_logits, *mine[1], *theirs[1])
+
+    rows = [v for k in range(2) for v in (*mine[k], *theirs[k])]
+    across = [swap(v, "c") for v in rows]
+    n_across = [swap(v, "c") for v in (n_low, n_high)]
 
     stat = lax.all_to_all(stat, "z", 0, 0, tiled=True)
+    stat, across = lax.optimization_barrier((stat, across))
     stat = call(middle_kernel, (sds((16, 16, LANE), F32),), (VMEM,), big=False)(stat)[0]
     stat = lax.all_to_all(stat, ("xh", "y", "xl"), 0, 0, tiled=True)
+    stat, n_across = lax.optimization_barrier((stat, n_across))
 
     mask = lax.dynamic_slice_in_dim(loss_mask, c * TOK, TOK, 0).astype(F32)[None, :]
     grads, kl = call(
@@ -551,13 +545,13 @@
         (sds((STEPS, LANE, TOK), BF16), sds((8, LANE), F32)),
         (SMEM,) + (VMEM,) * 6,
         big=False,
-    )(pos, stat, mask, early[0], early[1], l_last, targets)
+    )(pos, stat, mask, l_first, l_second, l_last, targets)
     grads_got, kl_got = swap(grads, "c"), swap(kl, "c")
 
     head_grad = call(
         head_kernel,
         (sds((32, LANE, LANE), BF16),),
-        (SMEM, VMEM, VMEM) + (ANY,) * 16,
+        (SMEM, VMEM, VMEM) + (ANY,) * 20,
         flops=2 * 768 * 4096 * 128,
         nbytes=8 << 20,
         scratch=[pltpu.VMEM((32, 768, LANE), BF16), pltpu.VMEM((32, LANE, LANE), BF16)]
@@ -567,12 +561,11 @@
         pos,
         grads,
         grads_got,
-        *mine[0],
-        *theirs[0],
-        *mine[1],
-        *theirs[1],
-        n_last,
+        *rows,
+        n_low,
+        n_high,
         *across,
+        *n_across,
     )[0].reshape(4096, LANE)
 
     blocks = TOK // BLK

time: 256 us -> 250 us (0.977)
  starting transfers between devices: 106 us -> 96.1 us
  waiting for transfers between devices: 88.5 us -> 98.1 us
  Pallas kernels: 41.7 us -> 37.5 us
    all_to_all x1, waiting for transfers between devices: 0.16 us -> 6.74 us  [on_device(): stat = lax.all_to_all(stat, ('xh', 'y', 'xl'), 0, 0, tiled=True)]
    all_to_all x2, waiting for transfers between devices: 21.1 us -> 27.5 us  [on_device(): rows = lax.all_to_all(mix, tp, 0, 0, tiled=True)]
    all_to_all x1, waiting for transfers between devices: 1.7 us -> 7.2 us  [on_device(): stat = lax.all_to_all(stat, 'z', 0, 0, tiled=True)]
    all_to_all x1, waiting for transfers between devices: 5.46 us -> 0.01 us  [on_device(): part = lax.all_to_all(mix, 'z', 0, 0, tiled=True).reshape(8 * HALF, LANE)]
    pallas_call x2 -> x1, Pallas kernels: 8.56 us -> 4.26 us  [on_device(): call(early_kernel, (sds((LANE, TOK), F32),), (SMEM,) + (ANY,) * 5, flops=...]
    ppermute x5, waiting for transfers between devices: 37.4 us -> 33.3 us  [across_grp(): return lax.ppermute(values, ('xh', 'xl'), list(pairs))]
    all_to_all x1, starting transfers between devices: 9.91 us -> 5.92 us  [on_device(): stat = lax.all_to_all(stat, 'z', 0, 0, tiled=True)]
    ppermute x2, waiting for transfers between devices: 1.79 us -> 4.74 us  [on_device(): ring += [lax.ppermute(a[0:1], 'z', up), lax.ppermute(b[1:2], 'z', down)]]
  transfers between devices with their start and end apart: 36 -> 39, of which waited for: 21 -> 19; matrix products, arithmetic and copies ran while one was open for 2% -> 2% of each run, Pallas kernels for 10% -> 10%
where the time goes in v3:
time: 250 us; the launch traced here: 249 us
  waiting for transfers between devices  98.1 us (39%)
  starting transfers between devices  96.1 us (38%)
  Pallas kernels  37.5 us (15%)
  local copies, waits for them, and re-layouts  12.2 us (5%)
  other arithmetic  3.72 us (1%)
    ppermute x5, waiting for transfers between devices, across_grp(): return lax.ppermute(values, ('xh', 'xl'), list(pairs))  33.3 us
    all_to_all x2, waiting for transfers between devices, on_device(): rows = lax.all_to_all(mix, tp, 0, 0, tiled=True)  27.5 us
    ppermute x15, starting transfers between devices, swap(): lax.ppermute(values, axis, [(i, (i + count // 2) % count) for i in range(...  20.8 us
    all_to_all x2, starting transfers between devices, on_device(): rows = lax.all_to_all(mix, tp, 0, 0, tiled=True)  17.8 us
    all_to_all x3, starting transfers between devices, spread(): lax.all_to_all(jnp.broadcast_to(values[None], (count,) + values.shape), a...  17.1 us
    pallas_call x2, Pallas kernels, on_device(): call(functools.partial(layer_kernel, step), (rows32, rows32, *kept, sds((...  8.51 us
    ppermute x6, waiting for transfers between devices, on_device(): a, b = (lax.ppermute(a, 'z', up), lax.ppermute(b, 'z', down))  8.33 us
    ppermute x3, starting transfers between devices, on_device(): lax.ppermute(mid, ('xh', 'y'), list(pairs))  7.59 us
  transfers between devices with their start and end apart: 39, of which 19 were waited for; matrix products, arithmetic and copies ran while one was open for 2% of the time, Pallas kernels for 10%

profile of v3, /device:TPU:1, one launch (start us, length us, event | category | flops | bytes accessed | tf_op | source)
XLA Modules:
  0.0 249.0 jit_solution(9122232832017156043)
XLA Ops:
  1.6 4.0 %collective-permute-start.1 = (bf16[128,128]{1,0:T(8,128)(2,1)S(1)}, bf16[128,128]{1,0:T(8,128)(2,1)S(1)}, u32[]{:S(2)}, u32[]{:S(2)}) collective-permute-start(bf16[128,128]{1,0:T(8,128)(2,1)S(1)} %get-tuple-element.94), channel_id=1, source_target_pairs={{0,32},{32,0},{192,224},{224,192},{1,33},{33,1},{193,225},{225,193... | collective-permute-start | bytes 98312 | tf_op jit(solution)/shard_map/ppermute | solution.py:409
  10.0 8.2 %all-to-all-start = ((bf16[8,128,128]{2,1,0:T(8,128)(2,1)}), bf16[8,128,128]{2,1,0:T(8,128)(2,1)S(1)}, u32[]{:S(2)}, u32[]{:S(2)}) async-start(bf16[8,128,128]{2,1,0:T(8,128)(2,1)} %broadcast_in_dim.74), calls=%async_computation | async-start | bytes 524288 | tf_op jit(solution)/shard_map/all_to_all | solution.py:55
  29.8 4.3 %all-to-all-start.1 = ((bf16[8,1024,128]{2,1,0:T(8,128)(2,1)}), bf16[8,1024,128]{2,1,0:T(8,128)(2,1)}, u32[]{:S(2)}, u32[]{:S(2)}) async-start(bf16[8,1024,128]{2,1,0:T(8,128)(2,1)} %broadcast_in_dim.82), calls=%async_computation.1 | async-start | bytes 4194304 | tf_op jit(solution)/shard_map/all_to_all | solution.py:55
  53.2 3.9 %collective-permute-done.11.rest_7_ = bf16[1,2,128,128]{3,2,1,0:T(8,128)(2,1)S(1)} collective-permute-done((bf16[1,2,128,128]{3,2,1,0:T(8,128)(2,1)S(1)}, bf16[1,2,128,128]{3,2,1,0:T(8,128)(2,1)S(1)}, u32[]{:S(2)}, u32[]{:S(2)}) %collective-permute-start.11) | collective-permute-done | bytes 65568 | tf_op jit(solution)/shard_map/ppermute | solution.py:431
  58.2 4.6 %shard_map.131 = (f32[64,128]{1,0:T(8,128)}, f32[64,128]{1,0:T(8,128)}) custom-call(s32[3]{0:T(128)} %pad_add_fusion.pos_ref, bf16[64,128,128]{2,1,0:T(8,128)(2,1)} %bitcast.12.a_ref.own_ref, bf16[2,2,128,128]{3,2,1,0:T(8,128)(2,1)} %copy-done.17, bf16[2,2,128,128]{3,2,1,0:T(8,128)(2,1)} %copy-done.21, bf16[2,2,128,128]{3,2,1,0:T(8,128)(2,1)} %copy-done.20, ...), custom_call_target="tpu_custom_call" | custom-call | flops 402653184 | bytes 6291456 | tf_op jit(solution)/shard_map/pallas_call | solution.py:433
  69.9 9.4 %all-to-all-start.2 = ((bf16[64,64,128]{2,1,0:T(8,128)(2,1)}), bf16[64,64,128]{2,1,0:T(8,128)(2,1)S(1)}, u32[]{:S(2)}, u32[]{:S(2)}) async-start(bf16[64,64,128]{2,1,0:T(8,128)(2,1)} %shard_map.132), calls=%async_computation.2 | async-start | bytes 2097152 | tf_op jit(solution)/shard_map/all_to_all | solution.py:466
  80.7 18.3 %all-to-all-done.2.far_x_ref = bf16[64,64,128]{2,1,0:T(8,128)(2,1)S(1)} async-done(((bf16[64,64,128]{2,1,0:T(8,128)(2,1)}), bf16[64,64,128]{2,1,0:T(8,128)(2,1)S(1)}, u32[]{:S(2)}, u32[]{:S(2)}) %all-to-all-start.2) | async-done | bytes 1048608 | tf_op jit(solution)/shard_map/all_to_all | solution.py:466
  100.0 4.5 %shard_map.133 = (bf16[32,64,128]{2,1,0:T(8,128)(2,1)}, bf16[32,64,128]{2,1,0:T(8,128)(2,1)}, f32[64,128]{1,0:T(8,128)}, bf16[64,128]{1,0:T(8,128)(2,1)}, bf16[64,64,128]{2,1,0:T(8,128)(2,1)}) custom-call(s32[3]{0:T(128)} %shifts_ref.7, bf16[64,64,128]{2,1,0:T(8,128)(2,1)} %copy-done.13, bf16[4,16,128]{2,1,0:T(8,128)(2,1)} %bitcast.36, ...), custom_call_target="tpu_custom_call" | custom-call | flops 134217728 | bytes 4194304 | tf_op jit(solution)/shard_map/pallas_call | solution.py:472
  104.5 8.5 %all-to-all-start.3 = ((bf16[64,64,128]{2,1,0:T(8,128)(2,1)}), bf16[64,64,128]{2,1,0:T(8,128)(2,1)S(1)}, u32[]{:S(2)}, u32[]{:S(2)}) async-start(bf16[64,64,128]{2,1,0:T(8,128)(2,1)} %get-tuple-element.51), calls=%async_computation.3 | async-start | bytes 2097152 | tf_op jit(solution)/shard_map/all_to_all | solution.py:466
  115.7 6.8 %collective-permute-done.14.got_ref = bf16[64,128,128]{2,1,0:T(8,128)(2,1)} collective-permute-done((bf16[64,128,128]{2,1,0:T(8,128)(2,1)}, bf16[64,128,128]{2,1,0:T(8,128)(2,1)}, u32[]{:S(2)}, u32[]{:S(2)}) %collective-permute-start.14) | collective-permute-done | bytes 2097184 | tf_op jit(solution)/shard_map/ppermute | solution.py:61
  122.5 9.2 %all-to-all-done.3.far_x_ref = bf16[64,64,128]{2,1,0:T(8,128)(2,1)S(1)} async-done(((bf16[64,64,128]{2,1,0:T(8,128)(2,1)}), bf16[64,64,128]{2,1,0:T(8,128)(2,1)S(1)}, u32[]{:S(2)}, u32[]{:S(2)}) %all-to-all-start.3) | async-done | bytes 1048608 | tf_op jit(solution)/shard_map/all_to_all | solution.py:466
  132.7 4.0 %shard_map.134 = (bf16[32,64,128]{2,1,0:T(8,128)(2,1)}, bf16[32,64,128]{2,1,0:T(8,128)(2,1)}, bf16[8,64,128]{2,1,0:T(8,128)(2,1)}) custom-call(s32[3]{0:T(128)} %shifts_ref.7, bf16[64,64,128]{2,1,0:T(8,128)(2,1)} %copy-done.12, bf16[4,16,128]{2,1,0:T(8,128)(2,1)} %bitcast.37, bf16[8192,128]{1,0:T(8,128)(2,1)} %far_w_ref.6, ...), custom_call_target="tpu_custom_call" | custom-call | flops 134217728 | bytes 4194304 | tf_op jit(solution)/shard_map/pallas_call | solution.py:472
  137.1 5.8 %all-to-all-start.4 = ((bf16[8,64,128]{2,1,0:T(8,128)(2,1)}), bf16[8,64,128]{2,1,0:T(8,128)(2,1)S(1)}, u32[]{:S(2)}, u32[]{:S(2)}) async-start(bf16[8,64,128]{2,1,0:T(8,128)(2,1)} %get-tuple-element.56), calls=%async_computation.4 | async-start | bytes 262144 | tf_op jit(solution)/shard_map/all_to_all | solution.py:487
  142.8 5.4 %shard_map.135.t_ref = f32[128,128]{1,0:T(8,128)} custom-call(s32[3]{0:T(128)} %pad_add_fusion.pos_ref, bf16[64,128,128]{2,1,0:T(8,128)(2,1)} %bitcast.12.a_ref.own_ref, bf16[64,128,128]{2,1,0:T(8,128)(2,1)} %collective-permute-done.14.got_ref, bf16[4,16,128]{2,1,0:T(8,128)(2,1)} %bitcast.40, bf16[8192,128]{1,0:T(8,128)(2,1)} %far_w_ref.7), custom_call_target="tpu_custom_call" | custom-call | flops 268435456 | bytes 4194304 | tf_op jit(solution)/shard_map/pallas_call | solution.py:488
  148.3 4.3 %shard_map.136.l0_ref.rest_0_ = f32[128,128]{1,0:T(8,128)} custom-call(s32[3]{0:T(128)} %pad_add_fusion.pos_ref, bf16[8192,128]{1,0:T(8,128)(2,1)} %far_w_ref.9, bf16[32,64,128]{2,1,0:T(8,128)(2,1)} %get-tuple-element.58.a_low_ref.rest_0_, bf16[32,64,128]{2,1,0:T(8,128)(2,1)} %get-tuple-element.61.a_high_ref.rest_1_, ...), custom_call_target="tpu_custom_call" | custom-call | flops 268435456 | bytes 4194304 | tf_op jit(solution)/shard_map/pallas_call | solution.py:499
  158.0 4.6 %all-to-all-start.5 = ((bf16[16,512,128]{2,1,0:T(8,128)(2,1)}), bf16[16,512,128]{2,1,0:T(8,128)(2,1)}, u32[]{:S(2)}, u32[]{:S(2)}) async-start(bf16[16,512,128]{2,1,0:T(8,128)(2,1)} %broadcast_in_dim.83), calls=%async_computation.5 | async-start | bytes 4194304 | tf_op jit(solution)/shard_map/all_to_all | solution.py:55
  165.1 8.7 %collective-permute-start.19 = (bf16[32,64,128]{2,1,0:T(8,128)(2,1)S(1)}, bf16[32,64,128]{2,1,0:T(8,128)(2,1)}, u32[]{:S(2)}, u32[]{:S(2)}) collective-permute-start(bf16[32,64,128]{2,1,0:T(8,128)(2,1)S(1)} %copy-done.14), channel_id=1, source_target_pairs={{0,1},{1,0},{2,3},{3,2},{4,5},{5,4},{6,7},{7,6},{8,9},{9,8},{10,11... | collective-permute-start | bytes 1572872 | tf_op jit(solution)/shard_map/ppermute | solution.py:66
  174.4 22.8 %collective-permute-done.18.rest_3_.rest_7_ = bf16[32,64,128]{2,1,0:T(8,128)(2,1)} collective-permute-done((bf16[32,64,128]{2,1,0:T(8,128)(2,1)}, bf16[32,64,128]{2,1,0:T(8,128)(2,1)}, u32[]{:S(2)}, u32[]{:S(2)}) %collective-permute-start.18) | collective-permute-done | bytes 524320 | tf_op jit(solution)/shard_map/ppermute | solution.py:61
  200.8 6.1 %shard_map.137 = (bf16[32,128,128]{2,1,0:T(8,128)(2,1)}, bf16[32,128,128]{2,1,0:T(8,128)(2,1)}, f32[128,128]{1,0:T(8,128)}, f32[128,128]{1,0:T(8,128)}, f32[3,128,128]{2,1,0:T(8,128)}, /*index=5*/f32[8,16,128]{2,1,0:T(8,128)}) custom-call(s32[3]{0:T(128)} %pad_add_fusion.pos_ref, s32[3]{0:T(128)} %shifts_ref.7, bf16[2,64,64,128]{3,2,1,0:T(8,128)(2,1)} %bitcast.17.far_x_ref, ...), custom_call_target="tpu_custom_call" | custom-call | flops 268435456 | bytes 6291456 | tf_op jit(solution)/shard_map/pallas_call | solution.py:514
  208.4 5.9 %all-to-all-start.6 = ((f32[8,16,128]{2,1,0:T(8,128)}), f32[8,16,128]{2,1,0:T(8,128)S(1)}, u32[]{:S(2)}, u32[]{:S(2)}) async-start(f32[8,16,128]{2,1,0:T(8,128)} %get-tuple-element.68), calls=%async_computation.6 | async-start | bytes 131072 | tf_op jit(solution)/shard_map/all_to_all | solution.py:536
  214.3 7.2 %all-to-all-done.6.in_ref = f32[8,16,128]{2,1,0:T(8,128)S(1)} async-done(((f32[8,16,128]{2,1,0:T(8,128)}), f32[8,16,128]{2,1,0:T(8,128)S(1)}, u32[]{:S(2)}, u32[]{:S(2)}) %all-to-all-start.6) | async-done | bytes 65568 | tf_op jit(solution)/shard_map/all_to_all | solution.py:536
  222.2 4.9 %all-to-all-start.7 = ((f32[16,16,128]{2,1,0:T(8,128)}), f32[16,16,128]{2,1,0:T(8,128)S(1)}, u32[]{:S(2)}, u32[]{:S(2)}) async-start(f32[16,16,128]{2,1,0:T(8,128)} %shard_map.138), calls=%async_computation.7 | async-start | bytes 262144 | tf_op jit(solution)/shard_map/all_to_all | solution.py:539
  227.2 6.7 %all-to-all-done.7.in_ref = f32[16,16,128]{2,1,0:T(8,128)S(1)} async-done(((f32[16,16,128]{2,1,0:T(8,128)}), f32[16,16,128]{2,1,0:T(8,128)S(1)}, u32[]{:S(2)}, u32[]{:S(2)}) %all-to-all-start.7) | async-done | bytes 131104 | tf_op jit(solution)/shard_map/all_to_all | solution.py:539
  243.3 5.5 %shard_map.140 = bf16[32,128,128]{2,1,0:T(8,128)(2,1)} custom-call(s32[3]{0:T(128)} %pad_add_fusion.pos_ref, bf16[3,128,128]{2,1,0:T(8,128)(2,1)} %copy-done.6, bf16[3,128,128]{2,1,0:T(8,128)(2,1)} %copy-done.24, bf16[32,64,128]{2,1,0:T(8,128)(2,1)} %get-tuple-element.58.a_low_ref.rest_0_, bf16[32,64,128]{2,1,0:T(8,128)(2,1)} %get-tuple-element.61.a_high_ref.rest_1_, ...), custom_call_target="tpu_custom_call" | custom-call | flops 805306368 | bytes 8388608 | tf_op jit(solution)/shard_map/pallas_call | solution.py:551
  (153 shorter events, 74.2 us)
Async XLA Ops:
  1.6 18.3 %collective-permute-start.1 = (bf16[128,128]{1,0:T(8,128)(2,1)S(1)}, bf16[128,128]{1,0:T(8,128)(2,1)S(1)}, u32[]{:S(2)}, u32[]{:S(2)}) collective-permute-start(bf16[128,128]{1,0:T(8,128)(2,1)S(1)} %get-tuple-element.94), channel_id=1, source_target_pairs={{0,32},{32,0},{192,224},{224,192},{1,33},{33,1},{193,225},{225,193... | collective-permute-start | bytes 98312 | tf_op jit(solution)/shard_map/ppermute | solution.py:409
  5.6 14.3 %collective-permute-start.2 = (bf16[128,128]{1,0:T(8,128)(2,1)S(1)}, bf16[128,128]{1,0:T(8,128)(2,1)S(1)}, u32[]{:S(2)}, u32[]{:S(2)}) collective-permute-start(bf16[128,128]{1,0:T(8,128)(2,1)S(1)} %get-tuple-element.94), channel_id=1, source_target_pairs={{0,96},{32,64},{192,160},{224,128},{1,97},{33,65},{193,161},{225,1... | collective-permute-start | bytes 98312 | tf_op jit(solution)/shard_map/ppermute | solution.py:409
  7.7 12.2 %collective-permute-start = (bf16[128,128]{1,0:T(8,128)(2,1)S(1)}, bf16[128,128]{1,0:T(8,128)(2,1)S(1)}, u32[]{:S(2)}, u32[]{:S(2)}) collective-permute-start(bf16[128,128]{1,0:T(8,128)(2,1)S(1)} %get-tuple-element.94), channel_id=1, source_target_pairs={{0,64},{32,96},{192,128},{224,160},{1,65},{33,97},{193,129},{225,1... | collective-permute-start | bytes 98312 | tf_op jit(solution)/shard_map/ppermute | solution.py:409
  10.0 18.3 %all-to-all-start = ((bf16[8,128,128]{2,1,0:T(8,128)(2,1)}), bf16[8,128,128]{2,1,0:T(8,128)(2,1)S(1)}, u32[]{:S(2)}, u32[]{:S(2)}) async-start(bf16[8,128,128]{2,1,0:T(8,128)(2,1)} %broadcast_in_dim.74), calls=%async_computation | async-start | bytes 524288 | tf_op jit(solution)/shard_map/all_to_all | solution.py:55
  29.8 28.3 %all-to-all-start.1 = ((bf16[8,1024,128]{2,1,0:T(8,128)(2,1)}), bf16[8,1024,128]{2,1,0:T(8,128)(2,1)}, u32[]{:S(2)}, u32[]{:S(2)}) async-start(bf16[8,1024,128]{2,1,0:T(8,128)(2,1)} %broadcast_in_dim.82), calls=%async_computation.1 | async-start | bytes 4194304 | tf_op jit(solution)/shard_map/all_to_all | solution.py:55
  69.9 29.1 %all-to-all-start.2 = ((bf16[64,64,128]{2,1,0:T(8,128)(2,1)}), bf16[64,64,128]{2,1,0:T(8,128)(2,1)S(1)}, u32[]{:S(2)}, u32[]{:S(2)}) async-start(bf16[64,64,128]{2,1,0:T(8,128)(2,1)} %shard_map.132), calls=%async_computation.2 | async-start | bytes 2097152 | tf_op jit(solution)/shard_map/all_to_all | solution.py:466
  79.3 43.3 %collective-permute-start.14 = (bf16[64,128,128]{2,1,0:T(8,128)(2,1)}, bf16[64,128,128]{2,1,0:T(8,128)(2,1)}, u32[]{:S(2)}, u32[]{:S(2)}) collective-permute-start(bf16[64,128,128]{2,1,0:T(8,128)(2,1)} %bitcast.12.a_ref.own_ref), channel_id=1, source_target_pairs={{144,0},{128,16},{145,1},{129,17},{146,2},{130,18},{147,3},{131,19... | collective-permute-start | bytes 6291464 | tf_op jit(solution)/shard_map/ppermute | solution.py:61
  104.5 27.2 %all-to-all-start.3 = ((bf16[64,64,128]{2,1,0:T(8,128)(2,1)}), bf16[64,64,128]{2,1,0:T(8,128)(2,1)S(1)}, u32[]{:S(2)}, u32[]{:S(2)}) async-start(bf16[64,64,128]{2,1,0:T(8,128)(2,1)} %get-tuple-element.51), calls=%async_computation.3 | async-start | bytes 2097152 | tf_op jit(solution)/shard_map/all_to_all | solution.py:466
  113.0 35.3 %collective-permute-start.16 = (bf16[32,64,128]{2,1,0:T(8,128)(2,1)}, bf16[32,64,128]{2,1,0:T(8,128)(2,1)}, u32[]{:S(2)}, u32[]{:S(2)}) collective-permute-start(bf16[32,64,128]{2,1,0:T(8,128)(2,1)} %get-tuple-element.58.a_low_ref.rest_0_), channel_id=1, source_target_pairs={{0,144},{16,128},{128,16},{144,0},{1,145},{17,129},{129,17},{145,1... | collective-permute-start | bytes 1572872 | tf_op jit(solution)/shard_map/ppermute | solution.py:61
  113.3 35.0 %collective-permute-start.17 = (bf16[32,64,128]{2,1,0:T(8,128)(2,1)}, bf16[32,64,128]{2,1,0:T(8,128)(2,1)}, u32[]{:S(2)}, u32[]{:S(2)}) collective-permute-start(bf16[32,64,128]{2,1,0:T(8,128)(2,1)} %get-tuple-element.61.a_high_ref.rest_1_), channel_id=1, source_target_pairs={{0,144},{16,128},{128,16},{144,0},{1,145},{17,129},{129,17},{145,1... | collective-permute-start | bytes 1572872 | tf_op jit(solution)/shard_map/ppermute | solution.py:61
  136.7 19.5 %collective-permute-start.15 = (bf16[32,64,128]{2,1,0:T(8,128)(2,1)}, bf16[32,64,128]{2,1,0:T(8,128)(2,1)}, u32[]{:S(2)}, u32[]{:S(2)}) collective-permute-start(bf16[32,64,128]{2,1,0:T(8,128)(2,1)} %get-tuple-element.57.rest_0_.rest_4_), channel_id=1, source_target_pairs={{0,144},{16,128},{128,16},{144,0},{1,145},{17,129},{129,17},{145,1... | collective-permute-start | bytes 1572872 | tf_op jit(solution)/shard_map/ppermute | solution.py:61
  137.1 15.5 %all-to-all-start.4 = ((bf16[8,64,128]{2,1,0:T(8,128)(2,1)}), bf16[8,64,128]{2,1,0:T(8,128)(2,1)S(1)}, u32[]{:S(2)}, u32[]{:S(2)}) async-start(bf16[8,64,128]{2,1,0:T(8,128)(2,1)} %get-tuple-element.56), calls=%async_computation.4 | async-start | bytes 262144 | tf_op jit(solution)/shard_map/all_to_all | solution.py:487
  158.0 42.7 %all-to-all-start.5 = ((bf16[16,512,128]{2,1,0:T(8,128)(2,1)}), bf16[16,512,128]{2,1,0:T(8,128)(2,1)}, u32[]{:S(2)}, u32[]{:S(2)}) async-start(bf16[16,512,128]{2,1,0:T(8,128)(2,1)} %broadcast_in_dim.83), calls=%async_computation.5 | async-start | bytes 4194304 | tf_op jit(solution)/shard_map/all_to_all | solution.py:55
  162.6 34.6 %collective-permute-start.18 = (bf16[32,64,128]{2,1,0:T(8,128)(2,1)}, bf16[32,64,128]{2,1,0:T(8,128)(2,1)}, u32[]{:S(2)}, u32[]{:S(2)}) collective-permute-start(bf16[32,64,128]{2,1,0:T(8,128)(2,1)} %get-tuple-element.66.rest_1_.rest_5_), channel_id=1, source_target_pairs={{0,144},{16,128},{128,16},{144,0},{1,145},{17,129},{129,17},{145,1... | collective-permute-start | bytes 1572872 | tf_op jit(solution)/shard_map/ppermute | solution.py:61
  165.1 41.7 %collective-permute-start.19 = (bf16[32,64,128]{2,1,0:T(8,128)(2,1)S(1)}, bf16[32,64,128]{2,1,0:T(8,128)(2,1)}, u32[]{:S(2)}, u32[]{:S(2)}) collective-permute-start(bf16[32,64,128]{2,1,0:T(8,128)(2,1)S(1)} %copy-done.14), channel_id=1, source_target_pairs={{0,1},{1,0},{2,3},{3,2},{4,5},{5,4},{6,7},{7,6},{8,9},{9,8},{10,11... | collective-permute-start | bytes 1572872 | tf_op jit(solution)/shard_map/ppermute | solution.py:66
  173.8 33.1 %collective-permute-start.20 = (bf16[32,64,128]{2,1,0:T(8,128)(2,1)S(1)}, bf16[32,64,128]{2,1,0:T(8,128)(2,1)}, u32[]{:S(2)}, u32[]{:S(2)}) collective-permute-start(bf16[32,64,128]{2,1,0:T(8,128)(2,1)S(1)} %copy-done.15), channel_id=1, source_target_pairs={{0,1},{1,0},{2,3},{3,2},{4,5},{5,4},{6,7},{7,6},{8,9},{9,8},{10,11... | collective-permute-start | bytes 1572872 | tf_op jit(solution)/shard_map/ppermute | solution.py:66
  173.9 33.5 %collective-permute-start.22 = (bf16[32,64,128]{2,1,0:T(8,128)(2,1)}, bf16[32,64,128]{2,1,0:T(8,128)(2,1)}, u32[]{:S(2)}, u32[]{:S(2)}) collective-permute-start(bf16[32,64,128]{2,1,0:T(8,128)(2,1)} %collective-permute-done.17.b_high_ref.rest_3_), channel_id=1, source_target_pairs={{0,1},{1,0},{2,3},{3,2},{4,5},{5,4},{6,7},{7,6},{8,9},{9,8},{10,11... | collective-permute-start | bytes 1572872 | tf_op jit(solution)/shard_map/ppermute | solution.py:66
  174.3 33.2 %collective-permute-start.23 = (bf16[32,64,128]{2,1,0:T(8,128)(2,1)}, bf16[32,64,128]{2,1,0:T(8,128)(2,1)}, u32[]{:S(2)}, u32[]{:S(2)}) collective-permute-start(bf16[32,64,128]{2,1,0:T(8,128)(2,1)} %get-tuple-element.57.rest_0_.rest_4_), channel_id=1, source_target_pairs={{0,1},{1,0},{2,3},{3,2},{4,5},{5,4},{6,7},{7,6},{8,9},{9,8},{10,11... | collective-permute-start | bytes 1572872 | tf_op jit(solution)/shard_map/ppermute | solution.py:66
  197.2 10.7 %collective-permute-start.24 = (bf16[32,64,128]{2,1,0:T(8,128)(2,1)}, bf16[32,64,128]{2,1,0:T(8,128)(2,1)}, u32[]{:S(2)}, u32[]{:S(2)}) collective-permute-start(bf16[32,64,128]{2,1,0:T(8,128)(2,1)} %get-tuple-element.66.rest_1_.rest_5_), channel_id=1, source_target_pairs={{0,1},{1,0},{2,3},{3,2},{4,5},{5,4},{6,7},{7,6},{8,9},{9,8},{10,11... | collective-permute-start | bytes 1572872 | tf_op jit(solution)/shard_map/ppermute | solution.py:66
  206.8 27.1 %collective-permute-start.27 = (bf16[32,128,128]{2,1,0:T(8,128)(2,1)}, bf16[32,128,128]{2,1,0:T(8,128)(2,1)}, u32[]{:S(2)}, u32[]{:S(2)}) collective-permute-start(bf16[32,128,128]{2,1,0:T(8,128)(2,1)} %get-tuple-element.70.rest_8_), channel_id=1, source_target_pairs={{0,1},{1,0},{2,3},{3,2},{4,5},{5,4},{6,7},{7,6},{8,9},{9,8},{10,11... | collective-permute-start | bytes 3145736 | tf_op jit(solution)/shard_map/ppermute | solution.py:66
  206.9 27.0 %collective-permute-start.28 = (bf16[32,128,128]{2,1,0:T(8,128)(2,1)}, bf16[32,128,128]{2,1,0:T(8,128)(2,1)S(1)}, u32[]{:S(2)}, u32[]{:S(2)}) collective-permute-start(bf16[32,128,128]{2,1,0:T(8,128)(2,1)} %get-tuple-element.71.rest_9_), channel_id=1, source_target_pairs={{0,1},{1,0},{2,3},{3,2},{4,5},{5,4},{6,7},{7,6},{8,9},{9,8},{10,11... | collective-permute-start | bytes 3145736 | tf_op jit(solution)/shard_map/ppermute | solution.py:66
  207.4 6.8 %collective-permute-start.21 = (bf16[32,64,128]{2,1,0:T(8,128)(2,1)}, bf16[32,64,128]{2,1,0:T(8,128)(2,1)}, u32[]{:S(2)}, u32[]{:S(2)}) collective-permute-start(bf16[32,64,128]{2,1,0:T(8,128)(2,1)} %collective-permute-done.16.b_low_ref.rest_2_), channel_id=1, source_target_pairs={{0,1},{1,0},{2,3},{3,2},{4,5},{5,4},{6,7},{7,6},{8,9},{9,8},{10,11... | collective-permute-start | bytes 1572872 | tf_op jit(solution)/shard_map/ppermute | solution.py:66
  208.4 13.2 %all-to-all-start.6 = ((f32[8,16,128]{2,1,0:T(8,128)}), f32[8,16,128]{2,1,0:T(8,128)S(1)}, u32[]{:S(2)}, u32[]{:S(2)}) async-start(f32[8,16,128]{2,1,0:T(8,128)} %get-tuple-element.68), calls=%async_computation.6 | async-start | bytes 131072 | tf_op jit(solution)/shard_map/all_to_all | solution.py:536
  222.2 11.7 %all-to-all-start.7 = ((f32[16,16,128]{2,1,0:T(8,128)}), f32[16,16,128]{2,1,0:T(8,128)S(1)}, u32[]{:S(2)}, u32[]{:S(2)}) async-start(f32[16,16,128]{2,1,0:T(8,128)} %shard_map.138), calls=%async_computation.7 | async-start | bytes 262144 | tf_op jit(solution)/shard_map/all_to_all | solution.py:539
  (44 other events, 459.4 us)
